TPU v7x, 32 devices: a whole 2x2x4 slice. The times are simulated.
32 devices in a mesh: tm: 8 (over z, y), region: 4 (over x, core).
Axes of the slice: x: 2, y: 2, z: 4, core: 2. Of those that a mesh axis runs over, the one named last changes fastest.
Arguments:
- covariates: bfloat16 [8, 1024, 256], P('region', 'tm'), may hold values from -4 to 4
- observed: float32 [8, 1024, 256], P('region', 'tm'), may hold values from -40 to 40
- input_weight: bfloat16 [256, 256], replicated, may hold values from -0.375 to 0.375
- filter_weight: bfloat16 [3, 512, 512], replicated, may hold values from -0.25 to 0.25
- mixing_weight: bfloat16 [3, 256, 256], replicated, may hold values from -0.375 to 0.375
- output_weight: bfloat16 [256, 4096], replicated, may hold values from -0.375 to 0.375
Outputs:
- covariate_grad: bfloat16 [8, 1024, 256], P('region', 'tm')
- input_grad: bfloat16 [256, 256], P('tm')
- filter_grad: bfloat16 [3, 512, 512], P(None, 'tm')
- mixing_grad: bfloat16 [3, 256, 256], P(None, 'tm')
- output_grad: bfloat16 [256, 4096], P('tm')
All inputs are finite; a program needn't handle non-finite values.
Results may differ from a plain program's by a relative error of at most 0.022.
Values may be sent and summed in bfloat16 or wider, within the bound.
A program may use at most 64 MiB of HBM per device.

v0:
```python
import jax
import jax.numpy as jnp
from jax import lax
from jax.sharding import PartitionSpec as P

epsilon = 1e-05


def passed_along(block, axis, distance):
    devices = range(lax.axis_size(axis))
    route = [(i - distance, i) for i in devices if i - distance in devices]
    return lax.ppermute(block, axis, route)


def energy(predicted, observed, scenarios):
    node_count = observed.shape[-1]
    scenario_vals = predicted.reshape(predicted.shape[:-1] + (scenarios, node_count))
    gram_matrix = jnp.einsum(
        "...sn,...rn->...sr", scenario_vals, scenario_vals, precision=lax.Precision.HIGHEST
    )
    against = jnp.einsum(
        "...sn,...n->...s", scenario_vals, observed, precision=lax.Precision.HIGHEST
    )
    own_sq = jnp.diagonal(gram_matrix, axis1=-2, axis2=-1)
    target = jnp.sum(observed * observed, axis=-1)
    to_target = jnp.sqrt((own_sq - 2.0 * against + target[..., None]) / node_count + epsilon)
    off_diag = 1.0 - jnp.eye(scenarios, dtype=jnp.float32)
    pair_sq = (own_sq[..., :, None] + own_sq[..., None, :] - 2.0 * gram_matrix) / node_count
    between = jnp.sqrt(pair_sq * off_diag + epsilon) * off_diag
    return jnp.mean(to_target, axis=-1) - jnp.sum(between, axis=(-2, -1)) / (
        2.0 * scenarios * (scenarios - 1)
    )


def layer_forward(hidden, delayed, w_filter, w_mixing):
    channels = hidden.shape[-1]
    joined = jnp.concatenate([delayed, hidden], axis=-1)
    preact = jnp.dot(joined, w_filter, preferred_element_type=jnp.float32)
    gated = (jnp.tanh(preact[..., :channels]) * jax.nn.sigmoid(preact[..., channels:])).astype(
        jnp.bfloat16
    )
    result = (
        hidden.astype(jnp.float32) + jnp.dot(gated, w_mixing, preferred_element_type=jnp.float32)
    ).astype(jnp.bfloat16)
    return (result, (joined, preact, gated))


def layer_backward(grad_out, stored_layer, w_filter, w_mixing):
    joined, preact, gated = stored_layer
    channels = gated.shape[-1]
    upstream = grad_out.astype(jnp.float32)
    grad_mixing = jnp.einsum("btc,btd->cd", gated, upstream, preferred_element_type=jnp.float32)
    gated_cot = jnp.dot(upstream, w_mixing.T, preferred_element_type=jnp.float32).astype(
        jnp.bfloat16
    )
    grad_gated = lax.optimization_barrier(gated_cot).astype(jnp.float32)
    filter_act = jnp.tanh(preact[..., :channels])
    gate_act = jax.nn.sigmoid(preact[..., channels:])
    grad_preact = jnp.concatenate(
        [
            grad_gated * gate_act * (1.0 - filter_act * filter_act),
            grad_gated * filter_act * gate_act * (1.0 - gate_act),
        ],
        axis=-1,
    )
    grad_filter = jnp.einsum("btk,btj->kj", joined, grad_preact, preferred_element_type=jnp.float32)
    grad_joined = jnp.dot(grad_preact, w_filter.T, preferred_element_type=jnp.float32).astype(
        jnp.bfloat16
    )
    return (
        grad_joined[..., :channels],
        grad_joined[..., channels:],
        grad_out,
        grad_filter,
        grad_mixing,
    )


def per_device(covariates, observed, input_weight, filter_weight, mixing_weight, output_weight):
    batch_seqs, row_count, node_count = covariates.shape
    layer_total = filter_weight.shape[0]
    channels = mixing_weight.shape[1]
    scenarios = output_weight.shape[1] // node_count
    length = row_count * lax.axis_size("tm")
    local_sq = jnp.sum(observed * observed, axis=(1, 2))
    total_sq = lax.psum(local_sq, "tm")
    inv_scale = 1.0 / jnp.sqrt(total_sq / (length * node_count) + epsilon)
    hidden = jnp.dot(covariates, input_weight, preferred_element_type=jnp.float32).astype(
        jnp.bfloat16
    )
    stored = []
    for layer_no in range(layer_total):
        dilation = 2**layer_no
        incoming = passed_along(hidden[:, row_count - dilation :, :], "tm", 1)
        delayed = jnp.concatenate([incoming, hidden[:, : row_count - dilation, :]], axis=1)
        hidden, stored_layer = layer_forward(
            hidden, delayed, filter_weight[layer_no], mixing_weight[layer_no]
        )
        stored.append(stored_layer)
    predicted = jnp.dot(hidden, output_weight, preferred_element_type=jnp.float32)

    def scoring(values):
        return jnp.sum(energy(values, observed, scenarios) * inv_scale[:, None])

    _, pull_back = jax.vjp(scoring, predicted)
    (grad_pred,) = pull_back(jnp.ones((), jnp.float32))
    grad_output = jnp.einsum("btc,btj->cj", hidden, grad_pred, preferred_element_type=jnp.float32)
    grad_last = jnp.dot(grad_pred, output_weight.T, preferred_element_type=jnp.float32).astype(
        jnp.bfloat16
    )
    grad_hidden = grad_last
    filter_parts = [None] * layer_total
    mixing_parts = [None] * layer_total
    for layer_no in reversed(range(layer_total)):
        dilation = 2**layer_no
        grad_past, grad_now, grad_resid, grad_filter, grad_mixing = layer_backward(
            grad_hidden, stored[layer_no], filter_weight[layer_no], mixing_weight[layer_no]
        )
        extent = grad_past.shape[1]
        inside = jnp.concatenate(
            [grad_past[:, dilation:, :], jnp.zeros((batch_seqs, dilation, channels), jnp.bfloat16)],
            axis=1,
        )
        grad_hidden = grad_resid + grad_now + inside
        returned = passed_along(grad_past[:, :dilation, :], "tm", -1)
        grad_hidden = grad_hidden + jnp.concatenate(
            [jnp.zeros((batch_seqs, extent - dilation, channels), jnp.bfloat16), returned], axis=1
        )
        filter_parts[layer_no] = grad_filter
        mixing_parts[layer_no] = grad_mixing
    grad_input = jnp.einsum(
        "btn,btc->nc", covariates, grad_hidden, preferred_element_type=jnp.float32
    )
    covariate_grad = jnp.dot(
        grad_hidden, input_weight.T, preferred_element_type=jnp.float32
    ).astype(jnp.bfloat16)
    grad_filters = jnp.stack(filter_parts)
    grad_mixings = jnp.stack(mixing_parts)
    shares = (
        lax.psum_scatter(grad_input, "tm", scatter_dimension=0, tiled=True),
        lax.psum_scatter(grad_filters, "tm", scatter_dimension=1, tiled=True),
        lax.psum_scatter(grad_mixings, "tm", scatter_dimension=1, tiled=True),
        lax.psum_scatter(grad_output, "tm", scatter_dimension=0, tiled=True),
    )
    shares = (
        lax.psum(shares[0].astype(jnp.bfloat16), "region").astype(jnp.float32),
        lax.psum(shares[1].astype(jnp.bfloat16), "region").astype(jnp.float32),
        lax.psum(shares[2].astype(jnp.bfloat16), "region").astype(jnp.float32),
        lax.psum(shares[3].astype(jnp.bfloat16), "region").astype(jnp.float32),
    )
    shares = tuple((piece.astype(jnp.bfloat16) for piece in shares))
    return (covariate_grad, shares[0], shares[1], shares[2], shares[3])


def solution(mesh):
    placed = (P("region", "tm", None), P("region", "tm", None), P(), P(), P(), P())
    return jax.shard_map(
        per_device,
        mesh=mesh,
        in_specs=placed,
        out_specs=(
            P("region", "tm", None),
            P("tm", None),
            P(None, "tm", None),
            P(None, "tm", None),
            P("tm", None),
        ),
        check_vma=False,
    )
```

profile of v0, /device:TPU:0, one launch (start us, length us, event | category | flops | bytes accessed | tf_op | source)
XLA Modules:
  0.0 503.4 jit_solution(7413469068407177362)
XLA Ops:
  8.5 4.9 collective-permute-start
  13.4 1.7 multiply_reduce_fusion.1
  15.1 19.5 %psum.35 = f32[2]{0:T(128)S(1)} all-reduce(f32[2]{0:T(128)S(1)} %get-tuple-element.28), channel_id=1, replica_groups=mesh['tm'=8,'region'=4] {'tm'}, use_global_device_ids=true, to_apply=%region_2.3 | all-reduce | flops 2 | bytes 16 | tf_op jit(solution)/shard_map/psum | solution.py:86
  38.6 1.8 collective-permute-start.1
  43.0 4.2 collective-permute-start.2
  51.2 1.7 copy.95
  52.9 2.0 copy-done.1
  54.9 6.3 %fusion.6 = f32[2,128,16,16]{3,2,1,0:T(8,128)} fusion(f32[2,128,16,256]{3,2,1,0:T(8,128)S(1)} %bitcast.158), kind=kOutput, calls=%fused_computation.9 | convolution fusion | flops 201326592 | bytes 4456448 | tf_op jit(solution)/shard_map/jvp(...sn,...rn->...sr)/dot_general | solution.py:18
  61.2 2.3 copy.63
  63.6 3.2 copy.60
  66.8 6.5 %fusion.4 = f32[2,128,1,16]{3,2,1,0:T(1,128)} fusion(f32[2,128,256,1]{2,1,0,3:T(8,128)S(1)} %bitcast.163, f32[2,128,16,256]{3,2,1,0:T(8,128)} %bitcast.159), kind=kOutput, calls=%fused_computation.7 | convolution fusion | flops 12582912 | bytes 4472832 | tf_op jit(solution)/shard_map/jvp(...sn,...n->...s)/dot_general | solution.py:21
  74.8 1.7 gather_fusion
  82.5 2.1 copy.71
  84.6 6.9 %fusion = f32[2,128,16,256]{3,2,1,0:T(8,128)S(1)} fusion(f32[2,128,16,16]{3,2,1,0:T(8,128)} %copy.71, f32[2,128,16,256]{3,2,1,0:T(8,128)} %bitcast.160), kind=kOutput, calls=%fused_computation.3 | convolution fusion | flops 201326592 | bytes 8650752 | tf_op jit(solution)/shard_map/transpose(jvp(...sn,...rn->...sr))/dot_general | solution.py:18
  91.5 5.7 %add_add_fusion = bf16[2,128,16,256]{3,2,1,0:T(8,128)(2,1)} fusion(f32[2,128,16,256]{3,2,1,0:T(8,128)S(1)} %fusion, f32[2,128,16,16]{3,2,1,0:T(8,128)S(1)} %copy-done.3, f32[2,128,256]{2,1,0:T(8,128)S(1)} %copy-done.4, f32[2,128,16]{2,1,0:T(8,128)S(1)} %copy-done.19, f32[2,128,16,256]{3,2,1,0:T(8,128)S(1)} %bitcast.161), kind=kOutput, calls=%fused_computation.11 | convolution fusion | flops 205520896 | bytes 11026432 | tf_op jit(solution)/shard_map/transpose(jvp(...sn,...rn->...sr))/dot_general | solution.py:18
  97.3 4.2 reshape.36
  101.5 2.5 fusion.17
  106.1 4.4 collective-permute-done.3
  112.8 5.0 collective-permute-done.4
  120.9 4.1 collective-permute-done.5
  126.8 1.9 pad_maximum_fusion.1
  130.0 1.9 pad_maximum_fusion
  132.9 4.3 convolution_bitcast_fusion
  137.3 50.0 %reduce-scatter.13.cloned.1.call-done = f32[32,256]{1,0:T(8,128)} async-done(((f32[256,256]{1,0:T(8,128)}), f32[32,256]{1,0:T(8,128)}) %reduce-scatter.13.cloned.1.call-update) | async-done | bytes 32784
  188.7 64.1 %reduce-scatter.9.cloned.1.call-done = f32[3,32,256]{2,1,0:T(8,128)} async-done(((f32[3,256,256]{2,1,0:T(8,128)}), f32[3,32,256]{2,1,0:T(8,128)}) %reduce-scatter.9.cloned.1.call-update) | async-done | bytes 98320 | tf_op jit(solution)/shard_map/reduce_scatter | solution.py:142
  254.4 76.4 %reduce-scatter.7.cloned.1.call-done = f32[3,64,512]{2,1,0:T(8,128)} async-done(((f32[3,512,512]{2,1,0:T(8,128)}), f32[3,64,512]{2,1,0:T(8,128)}) %reduce-scatter.7.cloned.1.call-update) | async-done | bytes 393232 | tf_op jit(solution)/shard_map/reduce_scatter | solution.py:141
  330.8 1.7 convert_element_type.120
  332.5 89.4 %reduce-scatter.11.cloned.1.call-done = f32[32,4096]{1,0:T(8,128)} async-done(((f32[256,4096]{1,0:T(8,128)}), f32[32,4096]{1,0:T(8,128)}) %reduce-scatter.11.cloned.1.call-update) | async-done | bytes 524304 | tf_op jit(solution)/shard_map/reduce_scatter | solution.py:143
  421.9 1.8 convert_element_type.122
  424.6 29.9 %all-reduce.11.cloned.1.call-done = (bf16[32,256]{0,1:T(8,128)(2,1)}, bf16[3,32,256]{2,1,0:T(8,128)(2,1)}) async-done(((bf16[32,256]{0,1:T(8,128)(2,1)}, bf16[3,32,256]{2,1,0:T(8,128)(2,1)}), (bf16[32,256]{0,1:T(8,128)(2,1)}, bf16[3,32,256]{2,1,0:T(8,128)(2,1)})) %all-reduce.11.cloned.1.call-update) | async-done | bytes 65552 | tf_op jit(solution)/shard_map/psum | solution.py:146
  456.0 35.9 %all-reduce.13.cloned.1.call-done = (bf16[3,64,512]{2,1,0:T(8,128)(2,1)}, bf16[32,4096]{1,0:T(8,128)(2,1)}) async-done(((bf16[3,64,512]{2,1,0:T(8,128)(2,1)}, bf16[32,4096]{1,0:T(8,128)(2,1)}), (bf16[3,64,512]{2,1,0:T(8,128)(2,1)}, bf16[32,4096]{1,0:T(8,128)(2,1)})) %all-reduce.13.cloned.1.call-update) | async-done | bytes 458768 | tf_op jit(solution)/shard_map/psum | solution.py:147
  494.9 1.7 copy.113
  (155 shorter events, 38.8 us)
Async XLA Ops:
  7.2 43.2 %copy-start = (bf16[256,4096]{1,0:T(8,128)(2,1)S(1)}, bf16[256,4096]{1,0:T(8,128)(2,1)}, u32[]{:S(2)}) copy-start(bf16[256,4096]{1,0:T(8,128)(2,1)} %param.11) | copy-start | bytes 6291460
  7.2 180.1 %reduce-scatter.13.cloned.1.call-start = ((), (), s32[]{:S(2)}) async-start(), calls=%async_computation.7 | async-start | bytes 294912
  8.5 27.3 %collective-permute-start = (bf16[2,1,256]{2,1,0:T(2,128)(2,1)S(1)}, bf16[2,1,256]{2,1,0:T(2,128)(2,1)S(1)}, u32[]{:S(2)}, u32[]{:S(2)}) collective-permute-start(bf16[2,1,256]{2,1,0:T(2,128)(2,1)S(1)} %slice.133), channel_id=1, source_target_pairs={{0,4},{4,8},{8,12},{12,16},{16,20},{20,24},{24,28},{1,5},{5,9},{9,... | collective-permute-start | bytes 3080 | tf_op jit(solution)/shard_map/ppermute | solution.py:12
  34.7 7.6 %copy-start.38 = (bf16[3,512,512]{2,1,0:T(8,128)(2,1)S(1)}, bf16[3,512,512]{2,1,0:T(8,128)(2,1)}, u32[]{:S(2)}) copy-start(bf16[3,512,512]{2,1,0:T(8,128)(2,1)} %param.9) | copy-start | bytes 4718596
  35.9 6.9 %copy-start.9 = (bf16[3,256,256]{2,1,0:T(8,128)(2,1)S(1)}, bf16[3,256,256]{2,1,0:T(8,128)(2,1)}, u32[]{:S(2)}) copy-start(bf16[3,256,256]{2,1,0:T(8,128)(2,1)} %param.10) | copy-start | bytes 1179652
  37.4 4.3 copy-start.13
  38.6 3.1 collective-permute-start.1
  42.6 6.3 %copy-start.5 = (f32[2,128,512]{2,1,0:T(8,128)}, f32[2,128,512]{2,1,0:T(8,128)S(1)}, u32[]{:S(2)}) copy-start(f32[2,128,512]{2,1,0:T(8,128)S(1)} %fusion.24) | copy-start | bytes 1572868
  42.7 5.7 %copy-start.15 = (bf16[2,128,256]{2,1,0:T(8,128)(2,1)}, bf16[2,128,256]{2,1,0:T(8,128)(2,1)S(1)}, u32[]{:S(2)}) copy-start(bf16[2,128,256]{2,1,0:T(8,128)(2,1)S(1)} %multiply_convert_fusion.1) | copy-start | bytes 393220
  43.0 5.5 %collective-permute-start.2 = (bf16[2,4,256]{2,1,0:T(4,128)(2,1)S(1)}, bf16[2,4,256]{2,1,0:T(4,128)(2,1)S(1)}, u32[]{:S(2)}, u32[]{:S(2)}) collective-permute-start(bf16[2,4,256]{2,1,0:T(4,128)(2,1)S(1)} %slice.141), channel_id=1, source_target_pairs={{0,4},{4,8},{8,12},{12,16},{16,20},{20,24},{24,28},{1,5},{5,9},{9,... | collective-permute-start | bytes 12296 | tf_op jit(solution)/shard_map/ppermute | solution.py:12
  61.2 5.5 %copy-start.4 = (f32[2,128,256]{2,1,0:T(8,128)S(1)}, f32[2,128,256]{2,1,0:T(8,128)}, u32[]{:S(2)}) copy-start(f32[2,128,256]{2,1,0:T(8,128)} %param.7) | copy-start | bytes 786436
  84.6 6.9 %copy-start.2 = (f32[32,8,16,256]{3,2,1,0:T(8,128)S(1)}, f32[32,8,16,256]{3,2,1,0:T(8,128)}, u32[]{:S(2)}) copy-start(f32[32,8,16,256]{3,2,1,0:T(8,128)} %copy-done.1) | copy-start | bytes 12582916
  84.6 6.9 %copy-start.3 = (f32[2,128,16,16]{3,2,1,0:T(8,128)S(1)}, f32[2,128,16,16]{3,2,1,0:T(8,128)}, u32[]{:S(2)}) copy-start(f32[2,128,16,16]{3,2,1,0:T(8,128)} %copy.71) | copy-start | bytes 786436
  84.6 6.9 %copy-start.19 = (f32[2,128,16]{2,1,0:T(8,128)S(1)}, f32[2,128,16]{2,1,0:T(8,128)}, u32[]{:S(2)}) copy-start(f32[2,128,16]{2,1,0:T(8,128)} %copy.62) | copy-start | bytes 49156
  104.0 6.8 %copy-start.6 = (f32[2,128,512]{2,1,0:T(8,128)S(1)}, f32[2,128,512]{2,1,0:T(8,128)}, u32[]{:S(2)}) copy-start(f32[2,128,512]{2,1,0:T(8,128)} %copy-done.5) | copy-start | bytes 1572868
  104.4 7.0 %copy-start.21 = (bf16[2,128,256]{2,1,0:T(8,128)(2,1)}, bf16[2,128,256]{2,1,0:T(8,128)(2,1)S(1)}, u32[]{:S(2)}) copy-start(bf16[2,128,256]{2,1,0:T(8,128)(2,1)S(1)} %get-tuple-element.38) | copy-start | bytes 393220
  104.8 5.8 %collective-permute-start.3 = (bf16[2,4,256]{2,1,0:T(4,128)(2,1)S(1)}, bf16[2,4,256]{2,1,0:T(4,128)(2,1)S(1)}, u32[]{:S(2)}, u32[]{:S(2)}) collective-permute-start(bf16[2,4,256]{2,1,0:T(4,128)(2,1)S(1)} %slice.147), channel_id=1, source_target_pairs={{4,0},{8,4},{12,8},{16,12},{20,16},{24,20},{28,24},{5,1},{9,5},{13... | collective-permute-start | bytes 12296 | tf_op jit(solution)/shard_map/ppermute | solution.py:12
  111.0 7.6 %copy-start.25 = (bf16[2,128,256]{2,1,0:T(8,128)(2,1)}, bf16[2,128,256]{2,1,0:T(8,128)(2,1)S(1)}, u32[]{:S(2)}) copy-start(bf16[2,128,256]{2,1,0:T(8,128)(2,1)S(1)} %get-tuple-element.36) | copy-start | bytes 393220
  111.0 8.9 %copy-start.18 = (bf16[2,128,256]{2,1,0:T(8,128)(2,1)S(1)}, bf16[2,128,256]{2,1,0:T(8,128)(2,1)}, u32[]{:S(2)}) copy-start(bf16[2,128,256]{2,1,0:T(8,128)(2,1)} %copy-done.17) | copy-start | bytes 393220
  111.4 6.4 %collective-permute-start.4 = (bf16[2,2,256]{2,1,0:T(2,128)(2,1)S(1)}, bf16[2,2,256]{2,1,0:T(2,128)(2,1)S(1)}, u32[]{:S(2)}, u32[]{:S(2)}) collective-permute-start(bf16[2,2,256]{2,1,0:T(2,128)(2,1)S(1)} %slice.150), channel_id=1, source_target_pairs={{4,0},{8,4},{12,8},{16,12},{20,16},{24,20},{28,24},{5,1},{9,5},{13... | collective-permute-start | bytes 6152 | tf_op jit(solution)/shard_map/ppermute | solution.py:12
  117.8 7.3 %copy-start.31 = (bf16[2,128,256]{2,1,0:T(8,128)(2,1)S(1)}, bf16[2,128,256]{2,1,0:T(8,128)(2,1)}, u32[]{:S(2)}) copy-start(bf16[2,128,256]{2,1,0:T(8,128)(2,1)} %param.6) | copy-start | bytes 393220
  118.2 6.8 %copy-start.27 = (bf16[2,128,256]{2,1,0:T(8,128)(2,1)}, bf16[2,128,256]{2,1,0:T(8,128)(2,1)S(1)}, u32[]{:S(2)}) copy-start(bf16[2,128,256]{2,1,0:T(8,128)(2,1)S(1)} %get-tuple-element.33) | copy-start | bytes 393220
  118.3 6.8 %copy-start.29 = (bf16[2,128,256]{2,1,0:T(8,128)(2,1)}, bf16[2,128,256]{2,1,0:T(8,128)(2,1)S(1)}, u32[]{:S(2)}) copy-start(bf16[2,128,256]{2,1,0:T(8,128)(2,1)S(1)} %get-tuple-element.34) | copy-start | bytes 393220
  118.3 8.0 %copy-start.16 = (bf16[2,128,256]{2,1,0:T(8,128)(2,1)S(1)}, bf16[2,128,256]{2,1,0:T(8,128)(2,1)}, u32[]{:S(2)}) copy-start(bf16[2,128,256]{2,1,0:T(8,128)(2,1)} %copy-done.15) | copy-start | bytes 393220
  118.3 8.2 %copy-start.14 = (bf16[2,128,256]{2,1,0:T(8,128)(2,1)S(1)}, bf16[2,128,256]{2,1,0:T(8,128)(2,1)}, u32[]{:S(2)}) copy-start(bf16[2,128,256]{2,1,0:T(8,128)(2,1)} %copy-done.13) | copy-start | bytes 393220
  118.6 6.4 %collective-permute-start.5 = (bf16[2,1,256]{2,1,0:T(2,128)(2,1)S(1)}, bf16[2,1,256]{2,1,0:T(2,128)(2,1)S(1)}, u32[]{:S(2)}, u32[]{:S(2)}) collective-permute-start(bf16[2,1,256]{2,1,0:T(2,128)(2,1)S(1)} %slice.153), channel_id=1, source_target_pairs={{4,0},{8,4},{12,8},{16,12},{20,16},{24,20},{28,24},{5,1},{9,5},{13... | collective-permute-start | bytes 3080 | tf_op jit(solution)/shard_map/ppermute | solution.py:12
  126.2 126.6 %reduce-scatter.9.cloned.1.call-start = ((), (), s32[]{:S(2)}) async-start(), calls=%async_computation.5 | async-start | bytes 884736 | tf_op jit(solution)/shard_map/reduce_scatter | solution.py:142
  128.7 202.0 %reduce-scatter.7.cloned.1.call-start = ((), (), s32[]{:S(2)}) async-start(), calls=%async_computation.4 | async-start | bytes 3538944 | tf_op jit(solution)/shard_map/reduce_scatter | solution.py:141
  132.0 289.9 %reduce-scatter.11.cloned.1.call-start = ((), (), s32[]{:S(2)}) async-start(), calls=%async_computation.6 | async-start | bytes 4718592 | tf_op jit(solution)/shard_map/reduce_scatter | solution.py:143
  137.2 286.5 %copy-start.20 = (bf16[256,256]{1,0:T(8,128)(2,1)S(1)}, bf16[256,256]{1,0:T(8,128)(2,1)}, u32[]{:S(2)}) copy-start(bf16[256,256]{1,0:T(8,128)(2,1)} %param.8) | copy-start | bytes 393220
  137.2 317.3 %all-reduce.11.cloned.1.call-start = ((), (), s32[]{:S(2)}) async-start(), calls=%async_computation.8 | async-start | bytes 229376 | tf_op jit(solution)/shard_map/psum | solution.py:146
  254.4 237.5 %all-reduce.13.cloned.1.call-start = ((), (), s32[]{:S(2)}) async-start(), calls=%async_computation.9 | async-start | bytes 917504 | tf_op jit(solution)/shard_map/psum | solution.py:147
  (20 other events, 33.6 us)
Sparse Core Ops, SparseCore 0:
  126.3 60.8 reduce-scatter.12
  190.6 62.1 reduce-scatter.8
  256.9 73.8 reduce-scatter.6
  334.7 87.1 reduce-scatter.10
  424.7 29.7 all-reduce.10
  457.4 34.3 all-reduce.12
where the time goes:
time: 505 us; the launch traced here: 503 us
  waiting for transfers between devices  361 us (71%)
  matrix products  42.8 us (8%)
  local copies, waits for them, and re-layouts  32.5 us (6%)
  blocking collectives  19.5 us (4%)
  other arithmetic  18 us (4%)
  starting transfers between devices  15 us (3%)
  between operations  14.9 us (3%)
    reduce_scatter x1, waiting for transfers between devices, per_device(): lax.psum_scatter(grad_output, 'tm', scatter_dimension=0, tiled=True)  89.4 us
    reduce_scatter x1, waiting for transfers between devices, per_device(): lax.psum_scatter(grad_filters, 'tm', scatter_dimension=1, tiled=True)  76.4 us
    reduce_scatter x1, waiting for transfers between devices, per_device(): lax.psum_scatter(grad_mixings, 'tm', scatter_dimension=1, tiled=True)  64.1 us
    unnamed x7, waiting for transfers between devices  50.1 us
    psum x1, waiting for transfers between devices, per_device(): lax.psum(shares[1].astype(jnp.bfloat16), 'region').astype(jnp.float32)  35.9 us
    psum x1, waiting for transfers between devices, per_device(): lax.psum(shares[0].astype(jnp.bfloat16), 'region').astype(jnp.float32)  29.9 us
    psum x1, blocking collectives, per_device(): total_sq = lax.psum(local_sq, 'tm')  19.5 us
    dot_general x3, matrix products, energy(): jnp.einsum('...sn,...rn->...sr', scenario_vals, scenario_vals, precision=...  18.9 us
  transfers between devices with their start and end apart: 12, of which 11 were waited for; matrix products, arithmetic and copies ran while one was open for 5% of the time, Pallas kernels for 0%

commit v1 on v0

v1 whole, which is shorter than its diff:
```python
import functools

import jax
import jax.numpy as jnp
from jax import lax
from jax.experimental import pallas as pl
from jax.experimental.pallas import tpu as pltpu
from jax.sharding import PartitionSpec as P

MESH = pl.DeviceIdType.MESH
epsilon = 1e-05
HALO = 8
F32 = jnp.float32
BF16 = jnp.bfloat16


def dot(a, b, ca=1, cb=0, precision=None):
    return lax.dot_general(
        a, b, (((ca,), (cb,)), ((), ())), precision=precision, preferred_element_type=F32
    )


def edges_kernel(
    nt, cov, obs, prev_cov, next_cov, next_obs, total,
    got_prev, got_next, got_obs, sums, send_sem, recv_sem,
):
    me = lax.axis_index("tm")
    rows = cov.shape[1]

    def at(offset):
        return {"tm": lax.rem(me + offset, nt)}

    barrier = pltpu.get_barrier_semaphore()
    for offset in range(1, nt):
        pl.semaphore_signal(barrier, inc=1, device_id=at(offset), device_id_type=MESH)
    sq = obs[...] * obs[...]
    seqs, _, nodes = obs.shape
    sq = jnp.sum(sq.reshape(seqs, rows // 8, 8, nodes), axis=1)
    own = sq[:, :, :128]
    for part in range(1, nodes // 128):
        own = own + sq[:, :, part * 128 : (part + 1) * 128]
    sums[0] = own
    pl.semaphore_wait(barrier, nt - 1)
    copies = []

    def send(src, dst, offset):
        slot = len(copies)
        copy = pltpu.make_async_remote_copy(
            src_ref=src, dst_ref=dst, send_sem=send_sem.at[slot], recv_sem=recv_sem.at[slot],
            device_id=at(offset), device_id_type=MESH,
        )
        copy.start()
        copies.append(copy)

    send(cov.at[:, pl.ds(rows - 16, 16), :], got_prev, 1)
    send(cov.at[:, pl.ds(0, 16), :], got_next, nt - 1)
    send(obs.at[:, pl.ds(0, HALO), :], got_obs, nt - 1)
    for offset in range(1, nt):
        send(sums.at[0], sums.at[offset], offset)
    for copy in copies:
        copy.wait()
    prev_cov[...] = got_prev[...]
    next_cov[...] = got_next[...]
    next_obs[...] = got_obs[...]
    total[...] = jnp.sum(sums[...], axis=0)


def exchange_edges(nt, cov, obs):
    seqs, rows, nodes = cov.shape
    vmem = pl.BlockSpec(memory_space=pltpu.VMEM)
    edge = jax.ShapeDtypeStruct((seqs, 16, nodes), BF16)
    copies = nt + 2
    return pl.pallas_call(
        functools.partial(edges_kernel, nt),
        out_shape=(
            edge,
            edge,
            jax.ShapeDtypeStruct((seqs, HALO, nodes), F32),
            jax.ShapeDtypeStruct((seqs, 8, 128), F32),
        ),
        in_specs=[vmem] * 2,
        out_specs=(vmem,) * 4,
        scratch_shapes=[
            pltpu.VMEM((seqs, 16, nodes), BF16),
            pltpu.VMEM((seqs, 16, nodes), BF16),
            pltpu.VMEM((seqs, HALO, nodes), F32),
            pltpu.VMEM((nt, seqs, 8, 128), F32),
            pltpu.SemaphoreType.DMA((copies,)),
            pltpu.SemaphoreType.DMA((copies,)),
        ],
        compiler_params=pltpu.CompilerParams(collective_id=0, has_side_effects=True),
        name="edges",
    )(cov, obs)


def network_kernel(
    nt, packed,
    cov, obs, prev_cov, next_cov, next_obs, total, w_input, w_filter, w_mixing, w_output,
    cov_grad, *rest,
):
    if packed:
        grads, scen, scored = rest
    else:
        g_input, g_filter, g_mixing, g_output, scen, scored = rest
    me = lax.axis_index("tm")
    seqs, rows, nodes = cov.shape
    layers = w_filter.shape[0]
    channels = w_mixing.shape[1]
    scenarios = w_output.shape[1] // nodes
    span = rows + 2 * HALO
    kept = rows + HALO
    unit = channels // nt
    not_first = (me > 0).astype(F32)
    not_last = (me < nt - 1).astype(F32)

    def own_rows(x):
        return jnp.concatenate([x[b * span + HALO : b * span + HALO + rows] for b in range(seqs)], axis=0)

    def put(first_row, height, value):
        grads[:, first_row : first_row + height, :] = value.reshape(nt, height, nodes).astype(BF16)

    cov_own = cov[...]
    spans = []
    for b in range(seqs):
        spans.append(prev_cov[b].astype(F32)[16 - HALO :] * not_first)
        spans.append(cov_own[b].astype(F32))
        spans.append(next_cov[b].astype(F32)[:HALO])
    hidden = dot(jnp.concatenate(spans, axis=0).astype(BF16), w_input[...]).astype(BF16).astype(F32)
    stored = []
    for l in range(layers):
        delayed = pltpu.roll(hidden, 2**l, 0)
        joined = jnp.concatenate([delayed, hidden], axis=1).astype(BF16)
        preact = dot(joined, w_filter[l])
        act = jnp.tanh(preact[:, :channels])
        gate = 0.5 * jnp.tanh(0.5 * preact[:, channels:]) + 0.5
        gated = (act * gate).astype(BF16)
        stored.append((delayed, hidden, act, gate))
        hidden = (hidden + dot(gated, w_mixing[l])).astype(BF16).astype(F32)

    last = jnp.concatenate([hidden[b * span + HALO : (b + 1) * span] for b in range(seqs)], axis=0)
    last = last.astype(BF16)
    for s in range(scenarios):
        pred = dot(last, w_output[:, s * nodes : (s + 1) * nodes])
        for half in range(nodes // 128):
            scen[half, pl.ds(s, seqs * kept, stride=scenarios), :] = pred[:, half * 128 : (half + 1) * 128]
    for b in range(seqs):
        scored[b * kept : b * kept + rows] = obs[b]
        scored[b * kept + rows : (b + 1) * kept] = next_obs[b]

    block = 16 * scenarios
    row_no = lax.broadcasted_iota(jnp.int32, (block, block), 0)
    col_no = lax.broadcasted_iota(jnp.int32, (block, block), 1)
    same_step = (row_no // scenarios) == (col_no // scenarios)
    diagonal = row_no == col_no
    pairs = jnp.where(same_step & ~diagonal, 1.0 / (scenarios * (scenarios - 1) * nodes), 0.0)
    halves = nodes // 128

    def score(g, carry):
        at = pl.ds(pl.multiple_of(g * block, block), block)
        y = jnp.concatenate([scen[h, at, :] for h in range(halves)], axis=1)
        o = scored[pl.ds(pl.multiple_of(g * 16, 16), 16), :]
        o = jnp.broadcast_to(o[:, None, :], (16, scenarios, nodes)).reshape(block, nodes)
        gram = dot(y, y, 1, 1, lax.Precision.HIGHEST)
        own = jnp.where(diagonal, gram, 0.0)
        own_sq = jnp.sum(own, axis=1, keepdims=True) + jnp.sum(own, axis=0, keepdims=True)
        pair_sq = jnp.maximum(own_sq - 2.0 * gram, 0.0) * (1.0 / nodes)
        coef = pairs * lax.rsqrt(pair_sq + epsilon)
        mixed = dot(coef, y, 1, 0, lax.Precision.HIGHEST)
        diff = y - o
        target = lax.rsqrt(jnp.sum(diff * diff, axis=1, keepdims=True) * (1.0 / nodes) + epsilon)
        target = target * (1.0 / (scenarios * nodes))
        grad = mixed - jnp.sum(coef, axis=1, keepdims=True) * y + target * diff
        for h in range(halves):
            scen[h, at, :] = grad[:, h * 128 : (h + 1) * 128]
        return carry

    lax.fori_loop(0, seqs * kept // 16, score, 0)

    length = rows * nt
    step_no = lax.broadcasted_iota(jnp.int32, (kept, 1), 0)
    valid = jnp.where(step_no < rows, 1.0, not_last)
    factor = []
    for b in range(seqs):
        sq = jnp.sum(jnp.sum(total[b], axis=1, keepdims=True), axis=0, keepdims=True)
        factor.append(valid * lax.rsqrt(sq / (length * nodes) + epsilon))
    factor = jnp.concatenate(factor, axis=0)

    def kept_own(x):
        return jnp.concatenate([x[b * kept : b * kept + rows] for b in range(seqs)], axis=0)

    last_own = own_rows(hidden).T.astype(BF16)
    grad_last = jnp.zeros((seqs * kept, channels), F32)
    for s in range(scenarios):
        g = jnp.concatenate(
            [scen[h, pl.ds(s, seqs * kept, stride=scenarios), :] for h in range(halves)], axis=1
        )
        g = g * factor
        grad_last = grad_last + dot(g.astype(BF16), w_output[:, s * nodes : (s + 1) * nodes], 1, 1)
        part = dot(last_own, kept_own(g).astype(BF16))
        if packed:
            put(s * unit, unit, part)
        else:
            g_output[:, s * nodes : (s + 1) * nodes] = part.astype(BF16)
    grad_last = grad_last.astype(BF16).astype(F32)
    pieces = []
    for b in range(seqs):
        pieces.append(jnp.zeros((HALO, channels), F32))
        pieces.append(grad_last[b * kept : (b + 1) * kept])
    grad = jnp.concatenate(pieces, axis=0)

    first = scenarios * unit
    for l in reversed(range(layers)):
        delayed, held, act, gate = stored[l]
        grad16 = grad.astype(BF16)
        gated_t = own_rows(act * gate).T.astype(BF16)
        part = dot(gated_t, own_rows(grad).astype(BF16))
        if packed:
            put(first + layers * 4 * unit + l * unit, unit, part)
        else:
            g_mixing[l] = part.astype(BF16)
        gated_cot = dot(grad16, w_mixing[l], 1, 1).astype(BF16).astype(F32)
        pre = jnp.concatenate(
            [gated_cot * gate * (1.0 - act * act), gated_cot * act * gate * (1.0 - gate)], axis=1
        )
        own_pre = own_rows(pre).astype(BF16)
        for tap, source in enumerate((delayed, held)):
            part = dot(own_rows(source).T.astype(BF16), own_pre)
            if packed:
                owners = nt // 2
                height = 2 * unit
                for half in range(2):
                    piece = part[:, half * nodes : (half + 1) * nodes].reshape(owners, height, nodes)
                    at = first + (l * 2 + half) * height
                    grads[tap * owners : (tap + 1) * owners, at : at + height, :] = piece.astype(BF16)
            else:
                g_filter[l, tap * channels : (tap + 1) * channels, :] = part.astype(BF16)
        both = dot(pre.astype(BF16), w_filter[l], 1, 1).astype(BF16).astype(F32)
        past = pltpu.roll(both[:, :channels], seqs * span - 2**l, 0)
        grad = (grad + both[:, channels:] + past).astype(BF16).astype(F32)

    own = own_rows(grad).astype(BF16)
    cov_flat = jnp.concatenate([cov_own[b] for b in range(seqs)], axis=0)
    part = dot(cov_flat.astype(F32).T.astype(BF16), own)
    if packed:
        put(first + layers * 5 * unit, unit, part)
    else:
        g_input[...] = part.astype(BF16)
    result = dot(own, w_input[...], 1, 1).astype(BF16)
    for b in range(seqs):
        cov_grad[b] = result[b * rows : (b + 1) * rows]


def run_network(nt, packed, cov, obs, edges, weights):
    seqs, rows, nodes = cov.shape
    w_input, w_filter, w_mixing, w_output = weights
    scenarios = w_output.shape[1] // nodes
    vmem = pl.BlockSpec(memory_space=pltpu.VMEM)
    if packed:
        width = sum(w.size for w in weights) // nt // nodes
        grads = (jax.ShapeDtypeStruct((nt, width, nodes), BF16),)
    else:
        grads = tuple(jax.ShapeDtypeStruct(w.shape, BF16) for w in weights)
    steps = seqs * (rows + HALO)
    return pl.pallas_call(
        functools.partial(network_kernel, nt, packed),
        out_shape=(jax.ShapeDtypeStruct(cov.shape, BF16),) + grads,
        in_specs=[vmem] * 10,
        out_specs=(vmem,) * (1 + len(grads)),
        scratch_shapes=[
            pltpu.VMEM((nodes // 128, steps * scenarios, 128), F32),
            pltpu.VMEM((steps, nodes), F32),
        ],
        compiler_params=pltpu.CompilerParams(vmem_limit_bytes=56 * 2**20),
        name="network",
    )(cov, obs, *edges, *weights)


def plan(nt, nr, rows):
    bits = lambda n: n.bit_length() - 1
    tm_dims = [("tm", 2**i) for i in reversed(range(bits(nt)))]
    region_dims = [("region", 2**i) for i in reversed(range(bits(nr)))]
    near = region_dims[-1:]
    x, ys = region_dims[:-1], list(reversed(tm_dims))
    y, z = ys[:1], ys[1:]
    orders = [near + x + y + z, near + y + z[:1] + x + z[1:], near + z[:1] + x + y + z[1:]]
    units = rows // 16
    count = min(len(orders), units)
    cuts = [16 * (units * i // count) for i in range(count + 1)]
    parts = [(cuts[i], cuts[i + 1] - cuts[i], orders[i]) for i in range(count)]
    return tm_dims + region_dims, tm_dims, region_dims, parts


def reduce_kernel(nt, nr, rows, packed, shapes, grads, *refs):
    dims, tm_dims, region_dims, parts = plan(nt, nr, rows)
    n_out = len(shapes)
    outs, refs = refs[:n_out], list(refs[n_out:])
    send_sem, recv_sem = refs[-2:]
    whole = refs[-3]
    where = {"tm": lax.axis_index("tm"), "region": lax.axis_index("region")}

    def bit(dim):
        axis, weight = dim
        return lax.rem(lax.div(where[axis], weight), 2)

    def across(dim):
        axis, weight = dim
        return {axis: where[axis] + weight * (1 - 2 * bit(dim))}

    barrier = pltpu.get_barrier_semaphore()
    for dim in dims:
        pl.semaphore_signal(barrier, inc=1, device_id=across(dim), device_id_type=MESH)
    pl.semaphore_wait(barrier, len(dims))

    slot = 0
    state = []
    for i, (start, height, order) in enumerate(parts):
        buffers = refs[i * len(dims) : (i + 1) * len(dims)]
        state.append([grads, list(dims), buffers])

    def start_copy(src, dst, dim):
        nonlocal slot
        copy = pltpu.make_async_remote_copy(
            src_ref=src, dst_ref=dst, send_sem=send_sem.at[slot], recv_sem=recv_sem.at[slot],
            device_id=across(dim), device_id_type=MESH,
        )
        slot += 1
        copy.start()
        return copy

    def half(i, dim, side):
        left = state[i][1]
        rows_at = pl.ds(parts[i][0], parts[i][1]) if state[i][0] is grads else slice(None)
        return tuple(side if d == dim else slice(None) for d in left) + (rows_at, slice(None))

    def send_half(i, phase):
        dim = parts[i][2][phase]
        return start_copy(state[i][0].at[half(i, dim, 1 - bit(dim))], state[i][2][phase], dim)

    def gather_at(dim):
        place = region_dims.index(dim)
        return tuple(bit(d) if n <= place else slice(None) for n, d in enumerate(region_dims))

    def send_whole(i, n):
        dim = list(region_dims)[n]
        index = tuple(slice(None) if m < n else bit(d) for m, d in enumerate(region_dims))
        index = index + (pl.ds(parts[i][0], parts[i][1]), slice(None))
        return start_copy(whole.at[index], whole.at[index], dim)

    flying = [send_half(i, 0) for i in range(len(parts))]
    done = []
    for phase in range(len(dims)):
        for i in range(len(parts)):
            dim = parts[i][2][phase]
            flying[i].wait_recv()
            done.append(flying[i])
            source, left, buffers = state[i]
            into = buffers[phase]
            mine = source[half(i, dim, bit(dim))]
            into[...] = (into[...].astype(F32) + mine.astype(F32)).astype(BF16)
            state[i][0] = into
            state[i][1] = [d for d in left if d != dim]
            if phase + 1 < len(dims):
                flying[i] = send_half(i, phase + 1)
            else:
                index = tuple(bit(d) for d in region_dims)
                whole[index + (pl.ds(parts[i][0], parts[i][1]), slice(None))] = into[...]
                flying[i] = send_whole(i, 0)
    for n in range(len(region_dims)):
        for i in range(len(parts)):
            flying[i].wait_recv()
            done.append(flying[i])
            if n + 1 < len(region_dims):
                flying[i] = send_whole(i, n + 1)
    for copy in done:
        copy.wait_send()

    if not packed:
        outs[0][...] = whole[...]
        return

    def rows_of(first, height):
        sub, row = divmod(first, rows)
        index = []
        for axis, weight in region_dims:
            index.append(sub // weight % 2)
        return whole[tuple(index) + (slice(row, row + height), slice(None))]

    o_input, o_filter, o_mixing, o_output = outs
    unit, nodes = o_input.shape
    layers = o_filter.shape[0]
    scenarios = o_output.shape[1] // nodes
    for s in range(scenarios):
        o_output[:, s * nodes : (s + 1) * nodes] = rows_of(s * unit, unit)
    first = scenarios * unit
    for l in range(layers):
        for h in range(2):
            o_filter[l, :, h * nodes : (h + 1) * nodes] = rows_of(first + (l * 2 + h) * 2 * unit, 2 * unit)
        o_mixing[l] = rows_of(first + layers * 4 * unit + l * unit, unit)
    o_input[...] = rows_of(first + layers * 5 * unit, unit)


def reduce_grads(nt, nr, packed, grads, shapes):
    _, width, nodes = grads.shape
    rows = width // nr
    dims, tm_dims, region_dims, parts = plan(nt, nr, rows)
    grads = grads.reshape((2,) * len(dims) + (rows, nodes))
    whole = (2,) * len(region_dims) + (rows, nodes)
    if not packed:
        shapes = (whole,)
    vmem = pl.BlockSpec(memory_space=pltpu.VMEM)
    scratch = []
    for _, height, _ in parts:
        for phase in range(len(dims)):
            scratch.append(pltpu.VMEM((2,) * (len(dims) - phase - 1) + (height, nodes), BF16))
    copies = len(parts) * (len(dims) + len(region_dims))
    return pl.pallas_call(
        functools.partial(reduce_kernel, nt, nr, rows, packed, shapes),
        out_shape=tuple(jax.ShapeDtypeStruct(s, BF16) for s in shapes),
        in_specs=[vmem],
        out_specs=(vmem,) * len(shapes),
        scratch_shapes=scratch
        + [
            pltpu.VMEM(whole, BF16),
            pltpu.SemaphoreType.DMA((copies,)),
            pltpu.SemaphoreType.DMA((copies,)),
        ],
        compiler_params=pltpu.CompilerParams(
            collective_id=1, has_side_effects=True, vmem_limit_bytes=56 * 2**20
        ),
        name="reduce",
    )(grads)


def per_device(nt, nr, cov, obs, w_input, w_filter, w_mixing, w_output):
    nodes = cov.shape[2]
    weights = (w_input, w_filter, w_mixing, w_output)
    layers, channels = w_mixing.shape[:2]
    scenarios = w_output.shape[1] // nodes
    unit = channels // nt
    packed = unit % 16 == 0
    edges = exchange_edges(nt, cov, obs)
    cov_grad, *grads = run_network(nt, packed, cov, obs, edges, weights)
    shapes = (
        (unit, nodes), (layers, 2 * unit, 2 * channels), (layers, unit, channels), (unit, scenarios * nodes)
    )
    if packed:
        return (cov_grad,) + tuple(reduce_grads(nt, nr, True, grads[0], shapes))
    sources = tuple(
        jnp.moveaxis(g.reshape(g.shape[:-2] + (nt, -1) + g.shape[-1:]), -3, 0) for g in grads
    )
    flat = jnp.concatenate([s.reshape(nt, -1) for s in sources], axis=1).reshape(nt, -1, nodes)
    (summed,) = reduce_grads(nt, nr, False, flat, shapes)
    summed = summed.reshape(-1)
    outs, first = [], 0
    for source, shape in zip(sources, shapes):
        size = source.size // nt
        outs.append(summed[first : first + size].reshape(shape))
        first += size
    return (cov_grad, *outs)


def solution(mesh):
    placed = (P("region", "tm", None), P("region", "tm", None), P(), P(), P(), P())
    return jax.shard_map(
        functools.partial(per_device, mesh.shape["tm"], mesh.shape["region"]),
        mesh=mesh,
        in_specs=placed,
        out_specs=(
            P("region", "tm", None),
            P("tm", None),
            P(None, "tm", None),
            P(None, "tm", None),
            P("tm", None),
        ),
        check_vma=False,
    )
```

time: 505 us -> 88.6 us (0.18)
  waiting for transfers between devices: 361 us -> 0 us
  Pallas kernels: 0 us -> 81.6 us
  matrix products: 42.8 us -> 0 us
  local copies, waits for them, and re-layouts: 32.5 us -> 6.03 us
  blocking collectives: 19.5 us -> 0 us
  other arithmetic: 18 us -> 0 us
  starting transfers between devices: 15 us -> 0 us
  between operations: 14.9 us -> 0.65 us
    reduce_scatter x3 -> x0, waiting for transfers between devices: 230 us -> none  [the longest x1 89.4 us: per_device(): lax.psum_scatter(grad_output, 'tm', scatter_dimension=0, tiled=True)]
    pallas_call x0 -> x3, Pallas kernels: none -> 81.6 us  [the longest x1 38.1 us: reduce_grads(): pl.pallas_call(functools.partial(reduce_kernel, nt, nr, rows, packed, sha...]
    psum x2 -> x0, waiting for transfers between devices: 65.8 us -> none  [the longest x1 35.9 us: per_device(): lax.psum(shares[1].astype(jnp.bfloat16), 'region').astype(jnp.float32)]
    unnamed x7 -> x0, waiting for transfers between devices: 50.1 us -> none
    dot_general x28 -> x0, matrix products: 42.8 us -> none  [the longest x3 18.9 us: energy(): jnp.einsum('...sn,...rn->...sr', scenario_vals, scenario_vals, precision=...]
    psum x1 -> x0, blocking collectives: 19.5 us -> none  [per_device(): total_sq = lax.psum(local_sq, 'tm')]
    ppermute x6 -> x0, waiting for transfers between devices: 15 us -> none  [passed_along(): return lax.ppermute(block, axis, route)]
    ppermute x6 -> x0, starting transfers between devices: 14.8 us -> none  [passed_along(): return lax.ppermute(block, axis, route)]
  transfers between devices with their start and end apart: 12 -> 0, of which waited for: 11 -> 0; matrix products, arithmetic and copies ran while one was open for 5% -> 0% of each run, Pallas kernels for 0% -> 0%
where the time goes in v1:
time: 88.6 us; the launch traced here: 88.2 us
  Pallas kernels  81.6 us (92%)
  local copies, waits for them, and re-layouts  6.03 us (7%)
    pallas_call x1, Pallas kernels, reduce_grads(): pl.pallas_call(functools.partial(reduce_kernel, nt, nr, rows, packed, sha...  38.1 us
    pallas_call x1, Pallas kernels, run_network(): pl.pallas_call(functools.partial(network_kernel, nt, packed), out_shape=(...  32.7 us
    pallas_call x1, Pallas kernels, exchange_edges(): pl.pallas_call(functools.partial(edges_kernel, nt), out_shape=(edge, edge...  10.8 us
    unnamed x4, local copies, waits for them, and re-layouts  6.03 us

profile of v1, /device:TPU:0, one launch (start us, length us, event | category | flops | bytes accessed | tf_op | source)
XLA Modules:
  0.0 88.2 jit_solution(12186515246488534957)
XLA Ops:
  0.6 10.8 %edges.1 = (bf16[2,16,256]{2,1,0:T(8,128)(2,1)}, bf16[2,16,256]{2,1,0:T(8,128)(2,1)}, f32[2,8,256]{2,1,0:T(8,128)}, f32[2,8,128]{2,1,0:T(8,128)}) custom-call(bf16[2,128,256]{2,1,0:T(8,128)(2,1)} %cov.3, f32[2,128,256]{2,1,0:T(8,128)} %obs.3), custom_call_target="tpu_custom_call" | custom-call | tf_op jit(solution)/shard_map/edges/pallas_call | solution.py:73
  11.4 32.7 %network.1 = (bf16[2,128,256]{2,1,0:T(8,128)(2,1)}, bf16[8,1024,256]{2,1,0:T(8,128)(2,1)}) custom-call(bf16[2,128,256]{2,1,0:T(8,128)(2,1)} %cov.3, f32[2,128,256]{2,1,0:T(8,128)} %obs.3, bf16[2,16,256]{2,1,0:T(8,128)(2,1)} %get-tuple-element.15.prev_cov, bf16[2,16,256]{2,1,0:T(8,128)(2,1)} %get-tuple-element.16.next_cov, ...), custom_call_target="tpu_custom_call" | custom-call | tf_op jit(solution)/shard_map/network/pallas_call | solution.py:264
  44.1 38.1 %reduce.1 = (bf16[32,256]{1,0:T(8,128)(2,1)}, bf16[3,64,512]{2,1,0:T(8,128)(2,1)}, bf16[3,32,256]{2,1,0:T(8,128)(2,1)}, bf16[32,4096]{1,0:T(8,128)(2,1)}) custom-call(bf16[2,2,2,2,2,256,256]{6,5,4,3,2,1,0:T(8,128)(2,1)} %bitcast.1), custom_call_target="tpu_custom_call" | custom-call | tf_op jit(solution)/shard_map/reduce/pallas_call | solution.py:416
  82.2 1.3 %copy.15 = bf16[32,256]{1,0:T(8,128)(2,1)} copy(bf16[32,256]{1,0:T(8,128)(2,1)} %get-tuple-element.31) | data formatting | bytes 32768
  83.5 1.6 %copy.16 = bf16[3,64,512]{2,1,0:T(8,128)(2,1)} copy(bf16[3,64,512]{2,1,0:T(8,128)(2,1)} %get-tuple-element.32) | data formatting | bytes 393216
  85.1 1.4 %copy.17 = bf16[3,32,256]{2,1,0:T(8,128)(2,1)} copy(bf16[3,32,256]{2,1,0:T(8,128)(2,1)} %get-tuple-element.33) | data formatting | bytes 98304
  86.6 1.7 %copy.18 = bf16[32,4096]{1,0:T(8,128)(2,1)} copy(bf16[32,4096]{1,0:T(8,128)(2,1)} %get-tuple-element.34) | data formatting | bytes 524288

commit v2 on v1

--- a/solution.py
+++ b/solution.py
@@ -155,26 +155,44 @@
     pairs = jnp.where(same_step & ~diagonal, 1.0 / (scenarios * (scenarios - 1) * nodes), 0.0)
     halves = nodes // 128
 
-    def score(g, carry):
-        at = pl.ds(pl.multiple_of(g * block, block), block)
-        y = jnp.concatenate([scen[h, at, :] for h in range(halves)], axis=1)
-        o = scored[pl.ds(pl.multiple_of(g * 16, 16), 16), :]
-        o = jnp.broadcast_to(o[:, None, :], (16, scenarios, nodes)).reshape(block, nodes)
-        gram = dot(y, y, 1, 1, lax.Precision.HIGHEST)
-        own = jnp.where(diagonal, gram, 0.0)
-        own_sq = jnp.sum(own, axis=1, keepdims=True) + jnp.sum(own, axis=0, keepdims=True)
-        pair_sq = jnp.maximum(own_sq - 2.0 * gram, 0.0) * (1.0 / nodes)
-        coef = pairs * lax.rsqrt(pair_sq + epsilon)
-        mixed = dot(coef, y, 1, 0, lax.Precision.HIGHEST)
-        diff = y - o
-        target = lax.rsqrt(jnp.sum(diff * diff, axis=1, keepdims=True) * (1.0 / nodes) + epsilon)
-        target = target * (1.0 / (scenarios * nodes))
-        grad = mixed - jnp.sum(coef, axis=1, keepdims=True) * y + target * diff
-        for h in range(halves):
-            scen[h, at, :] = grad[:, h * 128 : (h + 1) * 128]
+    def score(groups):
+        ats = [pl.ds(pl.multiple_of(g * block, block), block) for g in groups]
+        ys = [jnp.concatenate([scen[h, at, :] for h in range(halves)], axis=1) for at in ats]
+        highs = [y.astype(BF16) for y in ys]
+        lows = [(y - hi.astype(F32)).astype(BF16) for y, hi in zip(ys, highs)]
+        grams = [
+            dot(jnp.concatenate([hi, lo, hi, lo], axis=1), jnp.concatenate([hi, hi, lo, lo], axis=1), 1, 1)
+            for hi, lo in zip(highs, lows)
+        ]
+        targets = []
+        for g, y in zip(groups, ys):
+            o = scored[pl.ds(pl.multiple_of(g * 16, 16), 16), :]
+            diff = y - jnp.broadcast_to(o[:, None, :], (16, scenarios, nodes)).reshape(block, nodes)
+            inv = lax.rsqrt(jnp.sum(diff * diff, axis=1, keepdims=True) * (1.0 / nodes) + epsilon)
+            targets.append(inv * (1.0 / (scenarios * nodes)) * diff)
+        coefs = []
+        for gram in grams:
+            own = jnp.where(diagonal, gram, 0.0)
+            own_sq = jnp.sum(own, axis=1, keepdims=True) + jnp.sum(own, axis=0, keepdims=True)
+            pair_sq = jnp.maximum(own_sq - 2.0 * gram, 0.0) * (1.0 / nodes)
+            coefs.append(pairs * lax.rsqrt(pair_sq + epsilon))
+        for at, y, hi, lo, coef, target in zip(ats, ys, highs, lows, coefs, targets):
+            chi = coef.astype(BF16)
+            clo = (coef - chi.astype(F32)).astype(BF16)
+            mixed = dot(jnp.concatenate([chi, clo, chi], axis=1), jnp.concatenate([hi, hi, lo], axis=0))
+            grad = mixed - jnp.sum(coef, axis=1, keepdims=True) * y + target
+            for h in range(halves):
+                scen[h, at, :] = grad[:, h * 128 : (h + 1) * 128]
+
+    groups = seqs * kept // 16
+
+    def score_pair(i, carry):
+        score([2 * i, 2 * i + 1])
         return carry
 
-    lax.fori_loop(0, seqs * kept // 16, score, 0)
+    lax.fori_loop(0, groups // 2, score_pair, 0)
+    if groups % 2:
+        score([groups - 1])
 
     length = rows * nt
     step_no = lax.broadcasted_iota(jnp.int32, (kept, 1), 0)
@@ -284,16 +302,14 @@
     y, z = ys[:1], ys[1:]
     orders = [near + x + y + z, near + y + z[:1] + x + z[1:], near + z[:1] + x + y + z[1:]]
     units = rows // 16
-    count = min(len(orders), units)
+    count = min(2 * len(orders), units)
     cuts = [16 * (units * i // count) for i in range(count + 1)]
-    parts = [(cuts[i], cuts[i + 1] - cuts[i], orders[i]) for i in range(count)]
+    parts = [(cuts[i], cuts[i + 1] - cuts[i], orders[i % 3]) for i in range(count)]
     return tm_dims + region_dims, tm_dims, region_dims, parts
 
 
-def reduce_kernel(nt, nr, rows, packed, shapes, grads, *refs):
+def reduce_kernel(nt, nr, rows, grads, out, *refs):
     dims, tm_dims, region_dims, parts = plan(nt, nr, rows)
-    n_out = len(shapes)
-    outs, refs = refs[:n_out], list(refs[n_out:])
     send_sem, recv_sem = refs[-2:]
     whole = refs[-3]
     where = {"tm": lax.axis_index("tm"), "region": lax.axis_index("region")}
@@ -374,18 +390,14 @@
     for copy in done:
         copy.wait_send()
 
-    if not packed:
-        outs[0][...] = whole[...]
-        return
-
+    out[...] = whole[...]
+
+
+def unpack_kernel(rows, whole, o_input, o_filter, o_mixing, o_output):
     def rows_of(first, height):
         sub, row = divmod(first, rows)
-        index = []
-        for axis, weight in region_dims:
-            index.append(sub // weight % 2)
-        return whole[tuple(index) + (slice(row, row + height), slice(None))]
-
-    o_input, o_filter, o_mixing, o_output = outs
+        return whole[sub, row : row + height, :]
+
     unit, nodes = o_input.shape
     layers = o_filter.shape[0]
     scenarios = o_output.shape[1] // nodes
@@ -399,14 +411,12 @@
     o_input[...] = rows_of(first + layers * 5 * unit, unit)
 
 
-def reduce_grads(nt, nr, packed, grads, shapes):
+def reduce_grads(nt, nr, grads):
     _, width, nodes = grads.shape
     rows = width // nr
     dims, tm_dims, region_dims, parts = plan(nt, nr, rows)
     grads = grads.reshape((2,) * len(dims) + (rows, nodes))
     whole = (2,) * len(region_dims) + (rows, nodes)
-    if not packed:
-        shapes = (whole,)
     vmem = pl.BlockSpec(memory_space=pltpu.VMEM)
     scratch = []
     for _, height, _ in parts:
@@ -414,10 +424,10 @@
             scratch.append(pltpu.VMEM((2,) * (len(dims) - phase - 1) + (height, nodes), BF16))
     copies = len(parts) * (len(dims) + len(region_dims))
     return pl.pallas_call(
-        functools.partial(reduce_kernel, nt, nr, rows, packed, shapes),
-        out_shape=tuple(jax.ShapeDtypeStruct(s, BF16) for s in shapes),
+        functools.partial(reduce_kernel, nt, nr, rows),
+        out_shape=jax.ShapeDtypeStruct(whole, BF16),
         in_specs=[vmem],
-        out_specs=(vmem,) * len(shapes),
+        out_specs=vmem,
         scratch_shapes=scratch
         + [
             pltpu.VMEM(whole, BF16),
@@ -428,7 +438,18 @@
             collective_id=1, has_side_effects=True, vmem_limit_bytes=56 * 2**20
         ),
         name="reduce",
-    )(grads)
+    )(grads).reshape(nr, rows, nodes)
+
+
+def unpack(summed, shapes):
+    vmem = pl.BlockSpec(memory_space=pltpu.VMEM)
+    return pl.pallas_call(
+        functools.partial(unpack_kernel, summed.shape[1]),
+        out_shape=tuple(jax.ShapeDtypeStruct(s, BF16) for s in shapes),
+        in_specs=[vmem],
+        out_specs=(vmem,) * len(shapes),
+        name="unpack",
+    )(summed)
 
 
 def per_device(nt, nr, cov, obs, w_input, w_filter, w_mixing, w_output):
@@ -444,13 +465,12 @@
         (unit, nodes), (layers, 2 * unit, 2 * channels), (layers, unit, channels), (unit, scenarios * nodes)
     )
     if packed:
-        return (cov_grad,) + tuple(reduce_grads(nt, nr, True, grads[0], shapes))
+        return (cov_grad, *unpack(reduce_grads(nt, nr, grads[0]), shapes))
     sources = tuple(
         jnp.moveaxis(g.reshape(g.shape[:-2] + (nt, -1) + g.shape[-1:]), -3, 0) for g in grads
     )
     flat = jnp.concatenate([s.reshape(nt, -1) for s in sources], axis=1).reshape(nt, -1, nodes)
-    (summed,) = reduce_grads(nt, nr, False, flat, shapes)
-    summed = summed.reshape(-1)
+    summed = reduce_grads(nt, nr, flat).reshape(-1)
     outs, first = [], 0
     for source, shape in zip(sources, shapes):
         size = source.size // nt

time: 88.6 us -> 69.8 us (0.79)
  Pallas kernels: 81.6 us -> 68.9 us
  local copies, waits for them, and re-layouts: 6.03 us -> 0 us
    pallas_call x1, Pallas kernels: 32.7 us -> 20.9 us  [run_network(): pl.pallas_call(functools.partial(network_kernel, nt, packed), out_shape=(...]
    unnamed x4 -> x0, local copies, waits for them, and re-layouts: 6.03 us -> none
    pallas_call x1 -> x2, Pallas kernels: 38.1 us -> 37.3 us  [the longest x1 35.4 us: reduce_grads(): pl.pallas_call(functools.partial(reduce_kernel, nt, nr, rows), out_shape=...]
where the time goes in v2:
time: 69.8 us; the launch traced here: 69.6 us
  Pallas kernels  68.9 us (99%)
    pallas_call x1, Pallas kernels, reduce_grads(): pl.pallas_call(functools.partial(reduce_kernel, nt, nr, rows), out_shape=...  35.4 us
    pallas_call x1, Pallas kernels, run_network(): pl.pallas_call(functools.partial(network_kernel, nt, packed), out_shape=(...  20.9 us
    pallas_call x1, Pallas kernels, exchange_edges(): pl.pallas_call(functools.partial(edges_kernel, nt), out_shape=(edge, edge...  10.8 us
    pallas_call x1, Pallas kernels, unpack(): pl.pallas_call(functools.partial(unpack_kernel, summed.shape[1]), out_sha...  1.83 us

profile of v2, /device:TPU:0, one launch (start us, length us, event | category | flops | bytes accessed | tf_op | source)
XLA Modules:
  0.0 69.6 jit_solution(7897569605812434756)
XLA Ops:
  0.6 10.8 %edges.1 = (bf16[2,16,256]{2,1,0:T(8,128)(2,1)}, bf16[2,16,256]{2,1,0:T(8,128)(2,1)}, f32[2,8,256]{2,1,0:T(8,128)}, f32[2,8,128]{2,1,0:T(8,128)}) custom-call(bf16[2,128,256]{2,1,0:T(8,128)(2,1)} %cov.3, f32[2,128,256]{2,1,0:T(8,128)} %obs.3), custom_call_target="tpu_custom_call" | custom-call | tf_op jit(solution)/shard_map/edges/pallas_call | solution.py:73
  11.4 20.9 %network.1 = (bf16[2,128,256]{2,1,0:T(8,128)(2,1)}, bf16[8,1024,256]{2,1,0:T(8,128)(2,1)}) custom-call(bf16[2,128,256]{2,1,0:T(8,128)(2,1)} %cov.3, f32[2,128,256]{2,1,0:T(8,128)} %obs.3, bf16[2,16,256]{2,1,0:T(8,128)(2,1)} %get-tuple-element.15.prev_cov, bf16[2,16,256]{2,1,0:T(8,128)(2,1)} %get-tuple-element.16.next_cov, ...), custom_call_target="tpu_custom_call" | custom-call | tf_op jit(solution)/shard_map/network/pallas_call | solution.py:282
  32.3 35.4 %reduce.1 = bf16[2,2,256,256]{3,2,1,0:T(8,128)(2,1)} custom-call(bf16[2,2,2,2,2,256,256]{6,5,4,3,2,1,0:T(8,128)(2,1)} %bitcast.2), custom_call_target="tpu_custom_call" | custom-call | tf_op jit(solution)/shard_map/reduce/pallas_call | solution.py:426
  67.7 1.8 %unpack.1 = (bf16[32,256]{1,0:T(8,128)(2,1)}, bf16[3,64,512]{2,1,0:T(8,128)(2,1)}, bf16[3,32,256]{2,1,0:T(8,128)(2,1)}, bf16[32,4096]{1,0:T(8,128)(2,1)}) custom-call(bf16[4,256,256]{2,1,0:T(8,128)(2,1)} %bitcast.3), custom_call_target="tpu_custom_call" | custom-call | tf_op jit(solution)/shard_map/unpack/pallas_call | solution.py:446

commit v3 on v2

v3 whole, which is shorter than its diff:
```python
import functools

import jax
import jax.numpy as jnp
from jax import lax
from jax.experimental import pallas as pl
from jax.experimental.pallas import tpu as pltpu
from jax.sharding import PartitionSpec as P

MESH = pl.DeviceIdType.MESH
epsilon = 1e-05
HALO = 8
F32 = jnp.float32
BF16 = jnp.bfloat16


def dot(a, b, ca=1, cb=0, precision=None):
    return lax.dot_general(
        a, b, (((ca,), (cb,)), ((), ())), precision=precision, preferred_element_type=F32
    )


class Edges:
    def __init__(self, nt, cov, obs, got_prev, got_next, got_obs, sums, send_sem, recv_sem):
        self.nt, self.cov, self.obs, self.sums = nt, cov, obs, sums
        self.got = (got_prev, got_next, got_obs)
        self.send_sem, self.recv_sem = send_sem, recv_sem
        self.copies = []

    def at(self, offset):
        return {"tm": lax.rem(lax.axis_index("tm") + offset, self.nt)}

    def greet(self, barrier):
        for offset in range(1, self.nt):
            pl.semaphore_signal(barrier, inc=1, device_id=self.at(offset), device_id_type=MESH)

    def own_squares(self):
        seqs, rows, nodes = self.obs.shape
        sq = self.obs[...] * self.obs[...]
        sq = jnp.sum(sq.reshape(seqs, rows // 8, 8, nodes), axis=1)
        own = sq[:, :, :128]
        for part in range(1, nodes // 128):
            own = own + sq[:, :, part * 128 : (part + 1) * 128]
        self.sums[0] = own

    def send(self, src, dst, offset):
        slot = len(self.copies)
        copy = pltpu.make_async_remote_copy(
            src_ref=src, dst_ref=dst,
            send_sem=self.send_sem.at[slot], recv_sem=self.recv_sem.at[slot],
            device_id=self.at(offset), device_id_type=MESH,
        )
        copy.start()
        self.copies.append(copy)

    def start(self):
        nt, rows = self.nt, self.cov.shape[1]
        self.send(self.cov.at[:, pl.ds(rows - 16, 16), :], self.got[0], 1)
        self.send(self.cov.at[:, pl.ds(0, 16), :], self.got[1], nt - 1)
        self.send(self.obs.at[:, pl.ds(0, HALO), :], self.got[2], nt - 1)
        for offset in range(1, nt):
            self.send(self.sums.at[0], self.sums.at[offset], offset)

    def arrived(self, first, last):
        for copy in self.copies[first:last]:
            copy.wait_recv()

    def sent(self):
        for copy in self.copies:
            copy.wait_send()

    def total(self):
        return jnp.sum(self.sums[...], axis=0)


def edges_kernel(nt, cov, obs, prev_cov, next_cov, next_obs, total, *scratch):
    edges = Edges(nt, cov, obs, *scratch)
    barrier = pltpu.get_barrier_semaphore()
    edges.greet(barrier)
    edges.own_squares()
    pl.semaphore_wait(barrier, nt - 1)
    edges.start()
    edges.arrived(0, None)
    edges.sent()
    for out, got in zip((prev_cov, next_cov, next_obs), edges.got):
        out[...] = got[...]
    total[...] = edges.total()


def exchange_edges(nt, cov, obs):
    seqs, rows, nodes = cov.shape
    vmem = pl.BlockSpec(memory_space=pltpu.VMEM)
    edge = jax.ShapeDtypeStruct((seqs, 16, nodes), BF16)
    copies = nt + 2
    return pl.pallas_call(
        functools.partial(edges_kernel, nt),
        out_shape=(
            edge,
            edge,
            jax.ShapeDtypeStruct((seqs, HALO, nodes), F32),
            jax.ShapeDtypeStruct((seqs, 8, 128), F32),
        ),
        in_specs=[vmem] * 2,
        out_specs=(vmem,) * 4,
        scratch_shapes=[
            pltpu.VMEM((seqs, 16, nodes), BF16),
            pltpu.VMEM((seqs, 16, nodes), BF16),
            pltpu.VMEM((seqs, HALO, nodes), F32),
            pltpu.VMEM((nt, seqs, 8, 128), F32),
            pltpu.SemaphoreType.DMA((copies,)),
            pltpu.SemaphoreType.DMA((copies,)),
        ],
        compiler_params=pltpu.CompilerParams(collective_id=0, has_side_effects=True),
        name="edges",
    )(cov, obs)


def network(
    nt, cov, obs, prev_cov, next_cov, next_obs, w_input, w_filter, w_mixing, w_output,
    cov_grad, scen, scored, need, emit, after,
):
    me = lax.axis_index("tm")
    seqs, rows, nodes = cov.shape
    layers = w_filter.shape[0]
    channels = w_mixing.shape[1]
    scenarios = w_output.shape[1] // nodes
    span = rows + 2 * HALO
    kept = rows + HALO
    not_first = (me > 0).astype(F32)
    not_last = (me < nt - 1).astype(F32)

    def own_rows(x):
        return jnp.concatenate([x[b * span + HALO : b * span + HALO + rows] for b in range(seqs)], axis=0)

    cov_own = cov[...]
    need("cov")
    need("input")
    spans = []
    for b in range(seqs):
        spans.append(prev_cov[b].astype(F32)[16 - HALO :] * not_first)
        spans.append(cov_own[b].astype(F32))
        spans.append(next_cov[b].astype(F32)[:HALO])
    hidden = dot(jnp.concatenate(spans, axis=0).astype(BF16), w_input[...]).astype(BF16).astype(F32)
    stored = []
    need("filter")
    need("mixing")
    for l in range(layers):
        delayed = pltpu.roll(hidden, 2**l, 0)
        joined = jnp.concatenate([delayed, hidden], axis=1).astype(BF16)
        preact = dot(joined, w_filter[l])
        act = jnp.tanh(preact[:, :channels])
        gate = 0.5 * jnp.tanh(0.5 * preact[:, channels:]) + 0.5
        gated = (act * gate).astype(BF16)
        stored.append((delayed, hidden, act, gate))
        hidden = (hidden + dot(gated, w_mixing[l])).astype(BF16).astype(F32)

    last = jnp.concatenate([hidden[b * span + HALO : (b + 1) * span] for b in range(seqs)], axis=0)
    last = last.astype(BF16)
    need("output")
    for s in range(scenarios):
        pred = dot(last, w_output[:, s * nodes : (s + 1) * nodes])
        for half in range(nodes // 128):
            scen[half, pl.ds(s, seqs * kept, stride=scenarios), :] = pred[:, half * 128 : (half + 1) * 128]
    need("obs")
    for b in range(seqs):
        scored[b * kept : b * kept + rows] = obs[b]
        scored[b * kept + rows : (b + 1) * kept] = next_obs[b]

    block = 16 * scenarios
    row_no = lax.broadcasted_iota(jnp.int32, (block, block), 0)
    col_no = lax.broadcasted_iota(jnp.int32, (block, block), 1)
    same_step = (row_no // scenarios) == (col_no // scenarios)
    diagonal = row_no == col_no
    pairs = jnp.where(same_step & ~diagonal, 1.0 / (scenarios * (scenarios - 1) * nodes), 0.0)
    halves = nodes // 128

    def score(groups):
        ats = [pl.ds(pl.multiple_of(g * block, block), block) for g in groups]
        ys = [jnp.concatenate([scen[h, at, :] for h in range(halves)], axis=1) for at in ats]
        highs = [y.astype(BF16) for y in ys]
        lows = [(y - hi.astype(F32)).astype(BF16) for y, hi in zip(ys, highs)]
        grams = [
            dot(jnp.concatenate([hi, lo, hi, lo], axis=1), jnp.concatenate([hi, hi, lo, lo], axis=1), 1, 1)
            for hi, lo in zip(highs, lows)
        ]
        targets = []
        for g, y in zip(groups, ys):
            o = scored[pl.ds(pl.multiple_of(g * 16, 16), 16), :]
            diff = y - jnp.broadcast_to(o[:, None, :], (16, scenarios, nodes)).reshape(block, nodes)
            inv = lax.rsqrt(jnp.sum(diff * diff, axis=1, keepdims=True) * (1.0 / nodes) + epsilon)
            targets.append(inv * (1.0 / (scenarios * nodes)) * diff)
        coefs = []
        for gram in grams:
            own = jnp.where(diagonal, gram, 0.0)
            own_sq = jnp.sum(own, axis=1, keepdims=True) + jnp.sum(own, axis=0, keepdims=True)
            pair_sq = jnp.maximum(own_sq - 2.0 * gram, 0.0) * (1.0 / nodes)
            coefs.append(pairs * lax.rsqrt(pair_sq + epsilon))
        for at, y, hi, lo, coef, target in zip(ats, ys, highs, lows, coefs, targets):
            chi = coef.astype(BF16)
            clo = (coef - chi.astype(F32)).astype(BF16)
            mixed = dot(jnp.concatenate([chi, clo, chi], axis=1), jnp.concatenate([hi, hi, lo], axis=0))
            grad = mixed - jnp.sum(coef, axis=1, keepdims=True) * y + target
            for h in range(halves):
                scen[h, at, :] = grad[:, h * 128 : (h + 1) * 128]

    groups = seqs * kept // 16

    def score_pair(i, carry):
        score([2 * i, 2 * i + 1])
        return carry

    lax.fori_loop(0, groups // 2, score_pair, 0)
    if groups % 2:
        score([groups - 1])

    length = rows * nt
    step_no = lax.broadcasted_iota(jnp.int32, (kept, 1), 0)
    valid = jnp.where(step_no < rows, 1.0, not_last)
    factor = []
    total = need("total")
    for b in range(seqs):
        sq = jnp.sum(jnp.sum(total[b], axis=1, keepdims=True), axis=0, keepdims=True)
        factor.append(valid * lax.rsqrt(sq / (length * nodes) + epsilon))
    factor = jnp.concatenate(factor, axis=0)

    def kept_own(x):
        return jnp.concatenate([x[b * kept : b * kept + rows] for b in range(seqs)], axis=0)

    last_own = own_rows(hidden).T.astype(BF16)
    grad_last = jnp.zeros((seqs * kept, channels), F32)
    for s in range(scenarios):
        g = jnp.concatenate(
            [scen[h, pl.ds(s, seqs * kept, stride=scenarios), :] for h in range(halves)], axis=1
        )
        g = g * factor
        grad_last = grad_last + dot(g.astype(BF16), w_output[:, s * nodes : (s + 1) * nodes], 1, 1)
        part = dot(last_own, kept_own(g).astype(BF16))
        emit("output", s, part)
    after("output")
    grad_last = grad_last.astype(BF16).astype(F32)
    pieces = []
    for b in range(seqs):
        pieces.append(jnp.zeros((HALO, channels), F32))
        pieces.append(grad_last[b * kept : (b + 1) * kept])
    grad = jnp.concatenate(pieces, axis=0)

    for l in reversed(range(layers)):
        delayed, held, act, gate = stored[l]
        grad16 = grad.astype(BF16)
        gated_t = own_rows(act * gate).T.astype(BF16)
        part = dot(gated_t, own_rows(grad).astype(BF16))
        emit("mixing", l, part)
        gated_cot = dot(grad16, w_mixing[l], 1, 1).astype(BF16).astype(F32)
        pre = jnp.concatenate(
            [gated_cot * gate * (1.0 - act * act), gated_cot * act * gate * (1.0 - gate)], axis=1
        )
        own_pre = own_rows(pre).astype(BF16)
        for tap, source in enumerate((delayed, held)):
            part = dot(own_rows(source).T.astype(BF16), own_pre)
            emit("filter", (l, tap), part)
        after(l)
        both = dot(pre.astype(BF16), w_filter[l], 1, 1).astype(BF16).astype(F32)
        past = pltpu.roll(both[:, :channels], seqs * span - 2**l, 0)
        grad = (grad + both[:, channels:] + past).astype(BF16).astype(F32)

    own = own_rows(grad).astype(BF16)
    cov_flat = jnp.concatenate([cov_own[b] for b in range(seqs)], axis=0)
    part = dot(cov_flat.astype(F32).T.astype(BF16), own)
    emit("input", None, part)
    after("input")
    result = dot(own, w_input[...], 1, 1).astype(BF16)
    for b in range(seqs):
        cov_grad[b] = result[b * rows : (b + 1) * rows]


def network_kernel(nt, cov, obs, prev_cov, next_cov, next_obs, total, *rest):
    weights, cov_grad, grads, (scen, scored) = rest[:4], rest[4], rest[5:9], rest[9:]
    g_input, g_filter, g_mixing, g_output = grads
    nodes, channels = cov.shape[2], weights[2].shape[1]

    def need(name):
        return total[...] if name == "total" else None

    def emit(name, index, part):
        part = part.astype(BF16)
        if name == "output":
            g_output[:, index * nodes : (index + 1) * nodes] = part
        elif name == "mixing":
            g_mixing[index] = part
        elif name == "filter":
            l, tap = index
            g_filter[l, tap * channels : (tap + 1) * channels, :] = part
        else:
            g_input[...] = part

    network(
        nt, cov, obs, prev_cov, next_cov, next_obs, *weights, cov_grad, scen, scored,
        need, emit, lambda stage: None,
    )


def network_scratch(cov, w_output):
    seqs, rows, nodes = cov.shape
    steps = seqs * (rows + HALO)
    scenarios = w_output.shape[1] // nodes
    return [
        pltpu.VMEM((nodes // 128, steps * scenarios, 128), F32),
        pltpu.VMEM((steps, nodes), F32),
    ]


def run_network(nt, cov, obs, edges, weights):
    vmem = pl.BlockSpec(memory_space=pltpu.VMEM)
    grads = tuple(jax.ShapeDtypeStruct(w.shape, BF16) for w in weights)
    return pl.pallas_call(
        functools.partial(network_kernel, nt),
        out_shape=(jax.ShapeDtypeStruct(cov.shape, BF16),) + grads,
        in_specs=[vmem] * 10,
        out_specs=(vmem,) * (1 + len(grads)),
        scratch_shapes=network_scratch(cov, weights[3]),
        compiler_params=pltpu.CompilerParams(vmem_limit_bytes=56 * 2**20),
        name="network",
    )(cov, obs, *edges, *weights)


def bit_dims(nt, nr):
    bits = lambda n: n.bit_length() - 1
    tm_dims = [("tm", 2**i) for i in reversed(range(bits(nt)))]
    region_dims = [("region", 2**i) for i in reversed(range(bits(nr)))]
    return tm_dims, region_dims


def orders_of(tm_dims, region_dims):
    near = region_dims[-1:]
    x, ys = region_dims[:-1], list(reversed(tm_dims))
    y, z = ys[:1], ys[1:]
    return [near + x + y + z, near + y + z[:1] + x + z[1:], near + z[:1] + x + y + z[1:]]


def even_parts(rows, orders):
    units = rows // 16
    count = min(2 * len(orders), units)
    cuts = [16 * (units * i // count) for i in range(count + 1)]
    return [(cuts[i], cuts[i + 1] - cuts[i], orders[i % 3]) for i in range(count)]


class Halving:
    def __init__(self, source, tm_dims, region_dims, parts, buffers, whole, send_sem, recv_sem):
        self.dims, self.region_dims, self.parts = tm_dims + region_dims, region_dims, parts
        self.source, self.whole = source, whole
        self.send_sem, self.recv_sem = send_sem, recv_sem
        n = len(self.dims)
        self.buffers = [buffers[i * n : (i + 1) * n] for i in range(len(parts))]
        self.current = [source for _ in parts]
        self.left = [list(self.dims) for _ in parts]
        self.phase = [0 for _ in parts]
        self.flying = [None for _ in parts]
        self.done = []
        self.slot = 0
        self.where = {"tm": lax.axis_index("tm"), "region": lax.axis_index("region")}

    def bit(self, dim):
        axis, weight = dim
        return lax.rem(lax.div(self.where[axis], weight), 2)

    def across(self, dim):
        axis, weight = dim
        return {axis: self.where[axis] + weight * (1 - 2 * self.bit(dim))}

    def copy(self, i, src, dst, dim):
        copy = pltpu.make_async_remote_copy(
            src_ref=src, dst_ref=dst,
            send_sem=self.send_sem.at[self.slot], recv_sem=self.recv_sem.at[self.slot],
            device_id=self.across(dim), device_id_type=MESH,
        )
        self.slot += 1
        copy.start()
        self.flying[i] = copy

    def rows_at(self, i):
        return pl.ds(self.parts[i][0], self.parts[i][1])

    def half(self, i, dim, side):
        rows = self.rows_at(i) if self.phase[i] == 0 else slice(None)
        return tuple(side if d == dim else slice(None) for d in self.left[i]) + (rows, slice(None))

    def send_half(self, i):
        dim = self.parts[i][2][self.phase[i]]
        at = self.half(i, dim, 1 - self.bit(dim))
        self.copy(i, self.current[i].at[at], self.buffers[i][self.phase[i]], dim)

    def send_whole(self, i, n):
        index = tuple(slice(None) if m < n else self.bit(d) for m, d in enumerate(self.region_dims))
        index = index + (self.rows_at(i), slice(None))
        self.copy(i, self.whole.at[index], self.whole.at[index], self.region_dims[n])

    def begin(self, i):
        self.send_half(i)

    def advance(self, i):
        if self.flying[i] is None:
            return False
        self.flying[i].wait_recv()
        self.done.append(self.flying[i])
        self.flying[i] = None
        phase, last = self.phase[i], len(self.dims)
        if phase < last:
            dim = self.parts[i][2][phase]
            into = self.buffers[i][phase]
            mine = self.current[i][self.half(i, dim, self.bit(dim))]
            into[...] = (into[...].astype(F32) + mine.astype(F32)).astype(BF16)
            self.current[i] = into
            self.left[i] = [d for d in self.left[i] if d != dim]
            self.phase[i] += 1
            if phase + 1 < last:
                self.send_half(i)
            else:
                index = tuple(self.bit(d) for d in self.region_dims)
                self.whole[index + (self.rows_at(i), slice(None))] = into[...]
                self.send_whole(i, 0)
        else:
            self.phase[i] += 1
            if phase + 1 - last < len(self.region_dims):
                self.send_whole(i, phase + 1 - last)
        return True

    def round(self):
        return any([self.advance(i) for i in range(len(self.parts))])

    def finish(self):
        while self.round():
            pass
        for copy in self.done:
            copy.wait_send()


def halving_scratch(tm_dims, region_dims, parts, rows, nodes):
    n = len(tm_dims) + len(region_dims)
    scratch = []
    for _, height, _ in parts:
        for phase in range(n):
            scratch.append(pltpu.VMEM((2,) * (n - phase - 1) + (height, nodes), BF16))
    copies = len(parts) * (n + len(region_dims))
    return scratch, [
        pltpu.VMEM((2,) * len(region_dims) + (rows, nodes), BF16),
        pltpu.SemaphoreType.DMA((copies,)),
        pltpu.SemaphoreType.DMA((copies,)),
    ]


def reduce_kernel(tm_dims, region_dims, parts, grads, out, *refs):
    halving = Halving(grads, tm_dims, region_dims, parts, refs[:-3], *refs[-3:])
    barrier = pltpu.get_barrier_semaphore()
    for dim in halving.dims:
        pl.semaphore_signal(barrier, inc=1, device_id=halving.across(dim), device_id_type=MESH)
    pl.semaphore_wait(barrier, len(halving.dims))
    for i in range(len(parts)):
        halving.begin(i)
    halving.finish()
    out[...] = halving.whole[...]


def reduce_grads(nt, nr, grads):
    _, width, nodes = grads.shape
    rows = width // nr
    tm_dims, region_dims = bit_dims(nt, nr)
    parts = even_parts(rows, orders_of(tm_dims, region_dims))
    grads = grads.reshape((2,) * (len(tm_dims) + len(region_dims)) + (rows, nodes))
    buffers, ends = halving_scratch(tm_dims, region_dims, parts, rows, nodes)
    vmem = pl.BlockSpec(memory_space=pltpu.VMEM)
    return pl.pallas_call(
        functools.partial(reduce_kernel, tm_dims, region_dims, parts),
        out_shape=jax.ShapeDtypeStruct((2,) * len(region_dims) + (rows, nodes), BF16),
        in_specs=[vmem],
        out_specs=vmem,
        scratch_shapes=buffers + ends,
        compiler_params=pltpu.CompilerParams(
            collective_id=1, has_side_effects=True, vmem_limit_bytes=56 * 2**20
        ),
        name="reduce",
    )(grads)


def staged_parts(unit, layers, per, orders):
    by_x, by_y, by_z = orders
    third = per * unit // 3 // 16 * 16
    early = per * unit - 2 * third
    parts, stages = [], {}

    def add(stage, start, height, order):
        stages.setdefault(stage, []).append(len(parts))
        parts.append((start, height, order))

    add("output", 0, early - (early - third) // 2 // 16 * 16, by_x)
    second = parts[0][1]
    add("output", second, per * unit - second - third, by_y)
    add("output", per * unit - third, third, by_z)
    cycle = [by_z, by_x, by_y]
    for n, l in enumerate(reversed(range(layers))):
        add(l, (per + n) * unit, unit, cycle[n % 3])
    tail = (per + layers) * unit
    cut = unit // 2 // 16 * 16
    if cut:
        add("input", tail, cut, by_y)
    add("input", tail + cut, unit - cut, by_z)
    return parts, stages


def step_kernel(
    nt, tm_dims, region_dims, parts, stages,
    cov, obs, w_input, w_filter, w_mixing, w_output, cov_grad, out,
    scen, scored, v_input, v_filter, v_mixing, v_output, load_sem, grads, *refs,
):
    edges = Edges(nt, cov, obs, *refs[:6])
    halving = Halving(grads, tm_dims, region_dims, parts, refs[6:-3], *refs[-3:])
    barrier = pltpu.get_barrier_semaphore()
    edges.greet(barrier)
    for dim in region_dims:
        pl.semaphore_signal(barrier, inc=1, device_id=halving.across(dim), device_id_type=MESH)
    loads = {}
    pairs = (("input", w_input, v_input), ("filter", w_filter, v_filter),
             ("mixing", w_mixing, v_mixing), ("output", w_output, v_output))
    for n, (name, src, dst) in enumerate(pairs):
        loads[name] = pltpu.make_async_copy(src, dst, load_sem.at[n])
        loads[name].start()
    edges.own_squares()
    pl.semaphore_wait(barrier, nt - 1 + len(region_dims))
    edges.start()

    nodes = cov.shape[2]
    layers, channels = w_mixing.shape[:2]
    unit = channels // nt
    per = w_output.shape[1] // nodes // 4
    every = (slice(None),) * len(tm_dims)

    def need(name):
        if name == "cov":
            edges.arrived(0, 2)
        elif name == "obs":
            edges.arrived(2, 3)
        elif name == "total":
            edges.arrived(3, None)
            return edges.total()
        else:
            loads[name].wait()

    def put(owners, sub, at, value):
        free = sum(1 for o in owners if isinstance(o, slice))
        index = owners + (sub // 2, sub % 2, slice(at * unit, (at + 1) * unit), slice(None))
        grads[index] = value.reshape((2,) * free + (unit, nodes)).astype(BF16)

    def emit(name, index, part):
        if name == "output":
            put(every, index // per, index % per, part)
        elif name == "mixing":
            put(every, index, per + layers, part)
        elif name == "input":
            put(every, layers, per + layers, part)
        else:
            l, tap = index
            for h in range(2):
                piece = part[:, h * nodes : (h + 1) * nodes].reshape(nt // 2, 2, unit, nodes)
                for q in range(2):
                    put((tap,) + every[1:], h * 2 + q, per + layers - 1 - l, piece[:, q])

    def after(stage):
        if stage != "output":
            halving.round()
        for i in stages.get(stage, []):
            halving.begin(i)

    network(
        nt, cov, obs, *edges.got, v_input, v_filter, v_mixing, v_output, cov_grad, scen, scored,
        need, emit, after,
    )
    halving.finish()
    edges.sent()
    out[...] = halving.whole[...]


def run_step(nt, nr, cov, obs, weights):
    seqs, rows, nodes = cov.shape
    w_input, w_filter, w_mixing, w_output = weights
    layers, channels = w_mixing.shape[:2]
    unit = channels // nt
    per = w_output.shape[1] // nodes // nr
    tm_dims, region_dims = bit_dims(nt, nr)
    parts, stages = staged_parts(unit, layers, per, orders_of(tm_dims, region_dims))
    chunk = (per + layers + 1) * unit
    buffers, ends = halving_scratch(tm_dims, region_dims, parts, chunk, nodes)
    vmem, anywhere = pl.BlockSpec(memory_space=pltpu.VMEM), pl.BlockSpec(memory_space=pl.ANY)
    dims = len(tm_dims) + len(region_dims)
    return pl.pallas_call(
        functools.partial(step_kernel, nt, tm_dims, region_dims, parts, stages),
        out_shape=(
            jax.ShapeDtypeStruct(cov.shape, BF16),
            jax.ShapeDtypeStruct((2,) * len(region_dims) + (chunk, nodes), BF16),
        ),
        in_specs=[vmem] * 2 + [anywhere] * 4,
        out_specs=(vmem, vmem),
        scratch_shapes=network_scratch(cov, w_output)
        + [pltpu.VMEM(w.shape, BF16) for w in weights]
        + [
            pltpu.SemaphoreType.DMA((4,)),
            pltpu.VMEM((2,) * dims + (chunk, nodes), BF16),
            pltpu.VMEM((seqs, 16, nodes), BF16),
            pltpu.VMEM((seqs, 16, nodes), BF16),
            pltpu.VMEM((seqs, HALO, nodes), F32),
            pltpu.VMEM((nt, seqs, 8, 128), F32),
            pltpu.SemaphoreType.DMA((nt + 2,)),
            pltpu.SemaphoreType.DMA((nt + 2,)),
        ]
        + buffers
        + ends,
        compiler_params=pltpu.CompilerParams(
            collective_id=2, has_side_effects=True, vmem_limit_bytes=56 * 2**20
        ),
        name="step",
    )(cov, obs, *weights)


def unpack_kernel(cov_grad, whole, o_cov, o_input, o_filter, o_mixing, o_output):
    unit, nodes = o_input.shape
    layers = o_filter.shape[0]
    scenarios = o_output.shape[1] // nodes
    per = scenarios // 4

    def piece(sub, at):
        return whole[sub // 2, sub % 2, at * unit : (at + 1) * unit, :]

    o_cov[...] = cov_grad[...]
    for s in range(scenarios):
        o_output[:, s * nodes : (s + 1) * nodes] = piece(s // per, s % per)
    for l in range(layers):
        for h in range(2):
            for q in range(2):
                o_filter[l, q * unit : (q + 1) * unit, h * nodes : (h + 1) * nodes] = piece(
                    h * 2 + q, per + layers - 1 - l
                )
        o_mixing[l] = piece(l, per + layers)
    o_input[...] = piece(layers, per + layers)


def unpack(cov_grad, summed, shapes):
    vmem = pl.BlockSpec(memory_space=pltpu.VMEM)
    shapes = (cov_grad.shape,) + shapes
    return pl.pallas_call(
        unpack_kernel,
        out_shape=tuple(jax.ShapeDtypeStruct(s, BF16) for s in shapes),
        in_specs=[vmem] * 2,
        out_specs=(vmem,) * len(shapes),
        name="unpack",
    )(cov_grad, summed)


def per_device(nt, nr, cov, obs, w_input, w_filter, w_mixing, w_output):
    nodes = cov.shape[2]
    weights = (w_input, w_filter, w_mixing, w_output)
    layers, channels = w_mixing.shape[:2]
    scenarios = w_output.shape[1] // nodes
    unit = channels // nt
    shapes = (
        (unit, nodes), (layers, 2 * unit, 2 * channels), (layers, unit, channels), (unit, scenarios * nodes)
    )
    if unit % 16 == 0 and nr == 4 and layers == 3 and scenarios % 4 == 0 and channels == nodes:
        return tuple(unpack(*run_step(nt, nr, cov, obs, weights), shapes))
    edges = exchange_edges(nt, cov, obs)
    cov_grad, *grads = run_network(nt, cov, obs, edges, weights)
    sources = tuple(
        jnp.moveaxis(g.reshape(g.shape[:-2] + (nt, -1) + g.shape[-1:]), -3, 0) for g in grads
    )
    flat = jnp.concatenate([s.reshape(nt, -1) for s in sources], axis=1).reshape(nt, -1, nodes)
    summed = reduce_grads(nt, nr, flat).reshape(-1)
    outs, first = [], 0
    for source, shape in zip(sources, shapes):
        size = source.size // nt
        outs.append(summed[first : first + size].reshape(shape))
        first += size
    return (cov_grad, *outs)


def solution(mesh):
    placed = (P("region", "tm", None), P("region", "tm", None), P(), P(), P(), P())
    return jax.shard_map(
        functools.partial(per_device, mesh.shape["tm"], mesh.shape["region"]),
        mesh=mesh,
        in_specs=placed,
        out_specs=(
            P("region", "tm", None),
            P("tm", None),
            P(None, "tm", None),
            P(None, "tm", None),
            P("tm", None),
        ),
        check_vma=False,
    )
```

time: 69.8 us -> 73.9 us (1.059); the launches traced: 69.6 us -> 72.8 us
  Pallas kernels: 68.9 us -> 72.1 us
    pallas_call x4 -> x2, Pallas kernels: 68.9 us -> 72.1 us  [the longest x1 70.2 us: run_step(): pl.pallas_call(functools.partial(step_kernel, nt, tm_dims, region_dims, p...]
where the time goes in v3:
time: 73.9 us; the launch traced here: 72.8 us
  Pallas kernels  72.1 us (98%)
    pallas_call x1, Pallas kernels, run_step(): pl.pallas_call(functools.partial(step_kernel, nt, tm_dims, region_dims, p...  70.2 us
    pallas_call x1, Pallas kernels, unpack(): pl.pallas_call(unpack_kernel, out_shape=tuple((jax.ShapeDtypeStruct(s, BF...  1.95 us

profile of v3, /device:TPU:0, one launch (start us, length us, event | category | flops | bytes accessed | tf_op | source)
XLA Modules:
  0.0 72.8 jit_solution(6955841750063341273)
XLA Ops:
  0.6 70.2 %step.1 = (bf16[2,128,256]{2,1,0:T(8,128)(2,1)}, bf16[2,2,256,256]{3,2,1,0:T(8,128)(2,1)}) custom-call(bf16[2,128,256]{2,1,0:T(8,128)(2,1)} %cov.1, f32[2,128,256]{2,1,0:T(8,128)} %obs.1, bf16[256,256]{1,0:T(8,128)(2,1)} %w_input.1, bf16[3,512,512]{2,1,0:T(8,128)(2,1)} %w_filter.1, bf16[3,256,256]{2,1,0:T(8,128)(2,1)} %w_mixing.1, bf16[256,4096]{1,0:T(8,128)(2,1)} %w_output.1), custom_call_target="tpu_custom_call" | custom-call | tf_op jit(solution)/shard_map/step/pallas_call | solution.py:593
  70.8 2.0 %unpack.1 = (bf16[2,128,256]{2,1,0:T(8,128)(2,1)}, bf16[32,256]{1,0:T(8,128)(2,1)}, bf16[3,64,512]{2,1,0:T(8,128)(2,1)}, bf16[3,32,256]{2,1,0:T(8,128)(2,1)}, bf16[32,4096]{1,0:T(8,128)(2,1)}) custom-call(bf16[2,128,256]{2,1,0:T(8,128)(2,1)} %get-tuple-element.7.cov_grad, bf16[2,2,256,256]{3,2,1,0:T(8,128)(2,1)} %get-tuple-element.8.whole), custom_call_target="tpu_custom_call" | custom-call | tf_op jit(solution)/shard_map/unpack/pallas_call | solution.py:647

commit v4 on v3

--- a/solution.py
+++ b/solution.py
@@ -126,6 +126,7 @@
     scenarios = w_output.shape[1] // nodes
     span = rows + 2 * HALO
     kept = rows + HALO
+    halves = nodes // 128
     not_first = (me > 0).astype(F32)
     not_last = (me < nt - 1).astype(F32)
 
@@ -157,10 +158,20 @@
     last = jnp.concatenate([hidden[b * span + HALO : (b + 1) * span] for b in range(seqs)], axis=0)
     last = last.astype(BF16)
     need("output")
-    for s in range(scenarios):
-        pred = dot(last, w_output[:, s * nodes : (s + 1) * nodes])
-        for half in range(nodes // 128):
-            scen[half, pl.ds(s, seqs * kept, stride=scenarios), :] = pred[:, half * 128 : (half + 1) * 128]
+    batch = 4 if scenarios % 4 == 0 else 1
+
+    def columns(s):
+        return pl.ds(pl.multiple_of(s * nodes, nodes), nodes)
+
+    def predict(j, carry):
+        for k in range(batch):
+            s = j * batch + k
+            pred = dot(last, w_output[:, columns(s)])
+            for h in range(halves):
+                scen[h, pl.ds(s, seqs * kept, stride=scenarios), :] = pred[:, h * 128 : (h + 1) * 128]
+        return carry
+
+    lax.fori_loop(0, scenarios // batch, predict, 0)
     need("obs")
     for b in range(seqs):
         scored[b * kept : b * kept + rows] = obs[b]
@@ -172,7 +183,6 @@
     same_step = (row_no // scenarios) == (col_no // scenarios)
     diagonal = row_no == col_no
     pairs = jnp.where(same_step & ~diagonal, 1.0 / (scenarios * (scenarios - 1) * nodes), 0.0)
-    halves = nodes // 128
 
     def score(groups):
         ats = [pl.ds(pl.multiple_of(g * block, block), block) for g in groups]
@@ -227,15 +237,20 @@
         return jnp.concatenate([x[b * kept : b * kept + rows] for b in range(seqs)], axis=0)
 
     last_own = own_rows(hidden).T.astype(BF16)
+
+    def output_step(j, grad_last):
+        for k in range(batch):
+            s = j * batch + k
+            g = jnp.concatenate(
+                [scen[h, pl.ds(s, seqs * kept, stride=scenarios), :] for h in range(halves)], axis=1
+            )
+            g = g * factor
+            grad_last = grad_last + dot(g.astype(BF16), w_output[:, columns(s)], 1, 1)
+            emit("output", (j, k), dot(last_own, kept_own(g).astype(BF16)))
+        return grad_last
+
     grad_last = jnp.zeros((seqs * kept, channels), F32)
-    for s in range(scenarios):
-        g = jnp.concatenate(
-            [scen[h, pl.ds(s, seqs * kept, stride=scenarios), :] for h in range(halves)], axis=1
-        )
-        g = g * factor
-        grad_last = grad_last + dot(g.astype(BF16), w_output[:, s * nodes : (s + 1) * nodes], 1, 1)
-        part = dot(last_own, kept_own(g).astype(BF16))
-        emit("output", s, part)
+    grad_last = lax.fori_loop(0, scenarios // batch, output_step, grad_last)
     after("output")
     grad_last = grad_last.astype(BF16).astype(F32)
     pieces = []
@@ -284,7 +299,9 @@
     def emit(name, index, part):
         part = part.astype(BF16)
         if name == "output":
-            g_output[:, index * nodes : (index + 1) * nodes] = part
+            j, k = index
+            batch = 4 if g_output.shape[1] // nodes % 4 == 0 else 1
+            g_output[:, pl.ds(pl.multiple_of((j * batch + k) * nodes, nodes), nodes)] = part
         elif name == "mixing":
             g_mixing[index] = part
         elif name == "filter":
@@ -345,14 +362,13 @@
 
 
 class Halving:
-    def __init__(self, source, tm_dims, region_dims, parts, buffers, whole, send_sem, recv_sem):
+    def __init__(self, sources, tm_dims, region_dims, parts, buffers, whole, send_sem, recv_sem):
         self.dims, self.region_dims, self.parts = tm_dims + region_dims, region_dims, parts
-        self.source, self.whole = source, whole
+        self.whole = whole
         self.send_sem, self.recv_sem = send_sem, recv_sem
         n = len(self.dims)
         self.buffers = [buffers[i * n : (i + 1) * n] for i in range(len(parts))]
-        self.current = [source for _ in parts]
-        self.left = [list(self.dims) for _ in parts]
+        self.current = list(sources)
         self.phase = [0 for _ in parts]
         self.flying = [None for _ in parts]
         self.done = []
@@ -380,14 +396,9 @@
     def rows_at(self, i):
         return pl.ds(self.parts[i][0], self.parts[i][1])
 
-    def half(self, i, dim, side):
-        rows = self.rows_at(i) if self.phase[i] == 0 else slice(None)
-        return tuple(side if d == dim else slice(None) for d in self.left[i]) + (rows, slice(None))
-
     def send_half(self, i):
         dim = self.parts[i][2][self.phase[i]]
-        at = self.half(i, dim, 1 - self.bit(dim))
-        self.copy(i, self.current[i].at[at], self.buffers[i][self.phase[i]], dim)
+        self.copy(i, self.current[i].at[1 - self.bit(dim)], self.buffers[i][self.phase[i]], dim)
 
     def send_whole(self, i, n):
         index = tuple(slice(None) if m < n else self.bit(d) for m, d in enumerate(self.region_dims))
@@ -407,10 +418,9 @@
         if phase < last:
             dim = self.parts[i][2][phase]
             into = self.buffers[i][phase]
-            mine = self.current[i][self.half(i, dim, self.bit(dim))]
+            mine = self.current[i][self.bit(dim)]
             into[...] = (into[...].astype(F32) + mine.astype(F32)).astype(BF16)
             self.current[i] = into
-            self.left[i] = [d for d in self.left[i] if d != dim]
             self.phase[i] += 1
             if phase + 1 < last:
                 self.send_half(i)
@@ -448,8 +458,9 @@
     ]
 
 
-def reduce_kernel(tm_dims, region_dims, parts, grads, out, *refs):
-    halving = Halving(grads, tm_dims, region_dims, parts, refs[:-3], *refs[-3:])
+def reduce_kernel(tm_dims, region_dims, parts, *refs):
+    sources, out, refs = refs[: len(parts)], refs[len(parts)], refs[len(parts) + 1 :]
+    halving = Halving(sources, tm_dims, region_dims, parts, refs[:-3], *refs[-3:])
     barrier = pltpu.get_barrier_semaphore()
     for dim in halving.dims:
         pl.semaphore_signal(barrier, inc=1, device_id=halving.across(dim), device_id_type=MESH)
@@ -466,19 +477,24 @@
     tm_dims, region_dims = bit_dims(nt, nr)
     parts = even_parts(rows, orders_of(tm_dims, region_dims))
     grads = grads.reshape((2,) * (len(tm_dims) + len(region_dims)) + (rows, nodes))
+    dims = tm_dims + region_dims
+    sources = []
+    for start, height, order in parts:
+        moved = tuple(dims.index(d) for d in order) + (len(dims), len(dims) + 1)
+        sources.append(jnp.transpose(grads[..., start : start + height, :], moved))
     buffers, ends = halving_scratch(tm_dims, region_dims, parts, rows, nodes)
     vmem = pl.BlockSpec(memory_space=pltpu.VMEM)
     return pl.pallas_call(
         functools.partial(reduce_kernel, tm_dims, region_dims, parts),
         out_shape=jax.ShapeDtypeStruct((2,) * len(region_dims) + (rows, nodes), BF16),
-        in_specs=[vmem],
+        in_specs=[vmem] * len(sources),
         out_specs=vmem,
         scratch_shapes=buffers + ends,
         compiler_params=pltpu.CompilerParams(
             collective_id=1, has_side_effects=True, vmem_limit_bytes=56 * 2**20
         ),
         name="reduce",
-    )(grads)
+    )(*sources)
 
 
 def staged_parts(unit, layers, per, orders):
@@ -495,24 +511,24 @@
     second = parts[0][1]
     add("output", second, per * unit - second - third, by_y)
     add("output", per * unit - third, third, by_z)
-    cycle = [by_z, by_x, by_y]
-    for n, l in enumerate(reversed(range(layers))):
-        add(l, (per + n) * unit, unit, cycle[n % 3])
-    tail = (per + layers) * unit
-    cut = unit // 2 // 16 * 16
-    if cut:
-        add("input", tail, cut, by_y)
-    add("input", tail + cut, unit - cut, by_z)
+    early_layers = (layers + 1) // 2
+    add(layers - early_layers, per * unit, early_layers * unit, by_z)
+    tail = (per + early_layers) * unit
+    rest = (layers + 1 - early_layers) * unit
+    cut = rest // 2 // 16 * 16
+    add("input", tail, cut, by_x)
+    add("input", tail + cut, rest - cut, by_y)
     return parts, stages
 
 
 def step_kernel(
     nt, tm_dims, region_dims, parts, stages,
     cov, obs, w_input, w_filter, w_mixing, w_output, cov_grad, out,
-    scen, scored, v_input, v_filter, v_mixing, v_output, load_sem, grads, *refs,
+    scen, scored, v_input, v_filter, v_mixing, v_output, load_sem, *refs,
 ):
     edges = Edges(nt, cov, obs, *refs[:6])
-    halving = Halving(grads, tm_dims, region_dims, parts, refs[6:-3], *refs[-3:])
+    sources, refs = refs[6 : 6 + len(parts)], refs[len(parts) :]
+    halving = Halving(sources, tm_dims, region_dims, parts, refs[6:-3], *refs[-3:])
     barrier = pltpu.get_barrier_semaphore()
     edges.greet(barrier)
     for dim in region_dims:
@@ -531,7 +547,7 @@
     layers, channels = w_mixing.shape[:2]
     unit = channels // nt
     per = w_output.shape[1] // nodes // 4
-    every = (slice(None),) * len(tm_dims)
+    every = range(nt)
 
     def need(name):
         if name == "cov":
@@ -545,26 +561,34 @@
             loads[name].wait()
 
     def put(owners, sub, at, value):
-        free = sum(1 for o in owners if isinstance(o, slice))
-        index = owners + (sub // 2, sub % 2, slice(at * unit, (at + 1) * unit), slice(None))
-        grads[index] = value.reshape((2,) * free + (unit, nodes)).astype(BF16)
+        value = value.reshape(len(owners), unit, nodes).astype(BF16)
+        place = {("region", 2): lax.div(sub, 2), ("region", 1): lax.rem(sub, 2)}
+        for source, (start, height, order) in zip(sources, parts):
+            low, high = max(start, at * unit), min(start + height, (at + 1) * unit)
+            if low >= high:
+                continue
+            for j, owner in enumerate(owners):
+                index = tuple(place[d] if d in place else owner // d[1] % 2 for d in order)
+                index = index + (slice(low - start, high - start), slice(None))
+                source[index] = value[j, low - at * unit : high - at * unit]
 
     def emit(name, index, part):
         if name == "output":
-            put(every, index // per, index % per, part)
+            put(every, index[0], index[1], part)
         elif name == "mixing":
             put(every, index, per + layers, part)
         elif name == "input":
             put(every, layers, per + layers, part)
         else:
             l, tap = index
+            owners = range(tap * nt // 2, (tap + 1) * nt // 2)
             for h in range(2):
                 piece = part[:, h * nodes : (h + 1) * nodes].reshape(nt // 2, 2, unit, nodes)
                 for q in range(2):
-                    put((tap,) + every[1:], h * 2 + q, per + layers - 1 - l, piece[:, q])
+                    put(owners, h * 2 + q, per + layers - 1 - l, piece[:, q])
 
     def after(stage):
-        if stage != "output":
+        if stage not in ("output", layers - 1):
             halving.round()
         for i in stages.get(stage, []):
             halving.begin(i)
@@ -602,7 +626,6 @@
         + [pltpu.VMEM(w.shape, BF16) for w in weights]
         + [
             pltpu.SemaphoreType.DMA((4,)),
-            pltpu.VMEM((2,) * dims + (chunk, nodes), BF16),
             pltpu.VMEM((seqs, 16, nodes), BF16),
             pltpu.VMEM((seqs, 16, nodes), BF16),
             pltpu.VMEM((seqs, HALO, nodes), F32),
@@ -610,6 +633,7 @@
             pltpu.SemaphoreType.DMA((nt + 2,)),
             pltpu.SemaphoreType.DMA((nt + 2,)),
         ]
+        + [pltpu.VMEM((2,) * dims + (height, nodes), BF16) for _, height, _ in parts]
         + buffers
         + ends,
         compiler_params=pltpu.CompilerParams(
@@ -662,7 +686,7 @@
     shapes = (
         (unit, nodes), (layers, 2 * unit, 2 * channels), (layers, unit, channels), (unit, scenarios * nodes)
     )
-    if unit % 16 == 0 and nr == 4 and layers == 3 and scenarios % 4 == 0 and channels == nodes:
+    if unit % 16 == 0 and nr == 4 and layers == 3 and scenarios == 16 and channels == nodes:
         return tuple(unpack(*run_step(nt, nr, cov, obs, weights), shapes))
     edges = exchange_edges(nt, cov, obs)
     cov_grad, *grads = run_network(nt, cov, obs, edges, weights)

time: 73.9 us -> 72 us (0.974); the launches traced: 72.8 us -> 71.9 us
  Pallas kernels: 72.1 us -> 71.2 us
    pallas_call x1, Pallas kernels: 70.2 us -> 69.3 us  [run_step(): pl.pallas_call(functools.partial(step_kernel, nt, tm_dims, region_dims, p...]
where the time goes in v4:
time: 72 us; the launch traced here: 71.9 us
  Pallas kernels  71.2 us (99%)
    pallas_call x1, Pallas kernels, run_step(): pl.pallas_call(functools.partial(step_kernel, nt, tm_dims, region_dims, p...  69.3 us
    pallas_call x1, Pallas kernels, unpack(): pl.pallas_call(unpack_kernel, out_shape=tuple((jax.ShapeDtypeStruct(s, BF...  1.95 us

profile of v4, /device:TPU:0, one launch (start us, length us, event | category | flops | bytes accessed | tf_op | source)
XLA Modules:
  0.0 71.9 jit_solution(10147094870733661276)
XLA Ops:
  0.6 69.3 %step.1 = (bf16[2,128,256]{2,1,0:T(8,128)(2,1)}, bf16[2,2,256,256]{3,2,1,0:T(8,128)(2,1)}) custom-call(bf16[2,128,256]{2,1,0:T(8,128)(2,1)} %cov.1, f32[2,128,256]{2,1,0:T(8,128)} %obs.1, bf16[256,256]{1,0:T(8,128)(2,1)} %w_input.1, bf16[3,512,512]{2,1,0:T(8,128)(2,1)} %w_filter.1, bf16[3,256,256]{2,1,0:T(8,128)(2,1)} %w_mixing.1, bf16[256,4096]{1,0:T(8,128)(2,1)} %w_output.1), custom_call_target="tpu_custom_call" | custom-call | tf_op jit(solution)/shard_map/step/pallas_call | solution.py:617
  69.9 2.0 %unpack.1 = (bf16[2,128,256]{2,1,0:T(8,128)(2,1)}, bf16[32,256]{1,0:T(8,128)(2,1)}, bf16[3,64,512]{2,1,0:T(8,128)(2,1)}, bf16[3,32,256]{2,1,0:T(8,128)(2,1)}, bf16[32,4096]{1,0:T(8,128)(2,1)}) custom-call(bf16[2,128,256]{2,1,0:T(8,128)(2,1)} %get-tuple-element.7.cov_grad, bf16[2,2,256,256]{3,2,1,0:T(8,128)(2,1)} %get-tuple-element.8.whole), custom_call_target="tpu_custom_call" | custom-call | tf_op jit(solution)/shard_map/unpack/pallas_call | solution.py:671

commit v5 on v4

--- a/solution.py
+++ b/solution.py
@@ -351,7 +351,16 @@
     near = region_dims[-1:]
     x, ys = region_dims[:-1], list(reversed(tm_dims))
     y, z = ys[:1], ys[1:]
-    return [near + x + y + z, near + y + z[:1] + x + z[1:], near + z[:1] + x + y + z[1:]]
+
+    def twos(dims):
+        return [dims[i : i + 2] for i in range(0, len(dims), 2)]
+
+    orders = [
+        [near, x, y] + twos(z),
+        [near, y, x] + twos(z),
+        [near, z[:1], x, y + z[1:2]] + twos(z[2:]),
+    ]
+    return [[group for group in order if group] for order in orders]
 
 
 def even_parts(rows, orders):
@@ -363,14 +372,14 @@
 
 class Halving:
     def __init__(self, sources, tm_dims, region_dims, parts, buffers, whole, send_sem, recv_sem):
-        self.dims, self.region_dims, self.parts = tm_dims + region_dims, region_dims, parts
+        self.region_dims, self.parts = region_dims, parts
         self.whole = whole
         self.send_sem, self.recv_sem = send_sem, recv_sem
-        n = len(self.dims)
-        self.buffers = [buffers[i * n : (i + 1) * n] for i in range(len(parts))]
         self.current = list(sources)
+        buffers = list(buffers)
+        self.buffers = [[buffers.pop(0) for _ in order] for _, _, order in parts]
         self.phase = [0 for _ in parts]
-        self.flying = [None for _ in parts]
+        self.flying = [[] for _ in parts]
         self.done = []
         self.slot = 0
         self.where = {"tm": lax.axis_index("tm"), "region": lax.axis_index("region")}
@@ -379,78 +388,88 @@
         axis, weight = dim
         return lax.rem(lax.div(self.where[axis], weight), 2)
 
-    def across(self, dim):
-        axis, weight = dim
-        return {axis: self.where[axis] + weight * (1 - 2 * self.bit(dim))}
-
-    def copy(self, i, src, dst, dim):
+    def partners(self, group):
+        masks = range(1, 2 ** len(group))
+        return [[d for n, d in enumerate(group) if mask >> n & 1] for mask in masks]
+
+    def across(self, dims):
+        place = {}
+        for axis, weight in dims:
+            here = place.get(axis, self.where[axis])
+            place[axis] = here + weight * (1 - 2 * self.bit((axis, weight)))
+        return place
+
+    def greet(self, barrier):
+        met = {}
+        for group in [g for _, _, order in self.parts for g in order] + [self.region_dims]:
+            for dims in self.partners(group):
+                met[tuple(sorted(dims))] = dims
+        for key in sorted(met):
+            pl.semaphore_signal(barrier, inc=1, device_id=self.across(met[key]), device_id_type=MESH)
+        return len(met)
+
+    def copy(self, i, src, dst, dims):
         copy = pltpu.make_async_remote_copy(
             src_ref=src, dst_ref=dst,
             send_sem=self.send_sem.at[self.slot], recv_sem=self.recv_sem.at[self.slot],
-            device_id=self.across(dim), device_id_type=MESH,
+            device_id=self.across(dims), device_id_type=MESH,
         )
         self.slot += 1
         copy.start()
-        self.flying[i] = copy
-
-    def rows_at(self, i):
-        return pl.ds(self.parts[i][0], self.parts[i][1])
-
-    def send_half(self, i):
-        dim = self.parts[i][2][self.phase[i]]
-        self.copy(i, self.current[i].at[1 - self.bit(dim)], self.buffers[i][self.phase[i]], dim)
-
-    def send_whole(self, i, n):
-        index = tuple(slice(None) if m < n else self.bit(d) for m, d in enumerate(self.region_dims))
-        index = index + (self.rows_at(i), slice(None))
-        self.copy(i, self.whole.at[index], self.whole.at[index], self.region_dims[n])
-
-    def begin(self, i):
-        self.send_half(i)
+        self.flying[i].append(copy)
+
+    def send_part(self, i):
+        group = self.parts[i][2][self.phase[i]]
+        for n, dims in enumerate(self.partners(group)):
+            index = tuple(1 - self.bit(d) if d in dims else self.bit(d) for d in group)
+            self.copy(i, self.current[i].at[index], self.buffers[i][self.phase[i]].at[n], dims)
+
+    def send_sum(self, i):
+        start, height, _ = self.parts[i]
+        index = tuple(self.bit(d) for d in self.region_dims) + (pl.ds(start, height), slice(None))
+        self.whole[index] = self.current[i][...]
+        for dims in self.partners(self.region_dims):
+            self.copy(i, self.whole.at[index], self.whole.at[index], dims)
 
     def advance(self, i):
-        if self.flying[i] is None:
+        if not self.flying[i]:
             return False
-        self.flying[i].wait_recv()
-        self.done.append(self.flying[i])
-        self.flying[i] = None
-        phase, last = self.phase[i], len(self.dims)
-        if phase < last:
-            dim = self.parts[i][2][phase]
-            into = self.buffers[i][phase]
-            mine = self.current[i][self.bit(dim)]
-            into[...] = (into[...].astype(F32) + mine.astype(F32)).astype(BF16)
-            self.current[i] = into
-            self.phase[i] += 1
-            if phase + 1 < last:
-                self.send_half(i)
+        for copy in self.flying[i]:
+            copy.wait_recv()
+        self.done += self.flying[i]
+        self.flying[i] = []
+        phase, order = self.phase[i], self.parts[i][2]
+        self.phase[i] += 1
+        if phase < len(order):
+            buffer = self.buffers[i][phase]
+            total = self.current[i][tuple(self.bit(d) for d in order[phase])].astype(F32)
+            for n in range(buffer.shape[0]):
+                total = total + buffer[n].astype(F32)
+            buffer[0] = total.astype(BF16)
+            self.current[i] = buffer.at[0]
+            if phase + 1 < len(order):
+                self.send_part(i)
             else:
-                index = tuple(self.bit(d) for d in self.region_dims)
-                self.whole[index + (self.rows_at(i), slice(None))] = into[...]
-                self.send_whole(i, 0)
-        else:
-            self.phase[i] += 1
-            if phase + 1 - last < len(self.region_dims):
-                self.send_whole(i, phase + 1 - last)
+                self.send_sum(i)
         return True
 
-    def round(self):
-        return any([self.advance(i) for i in range(len(self.parts))])
-
     def finish(self):
-        while self.round():
+        while any([self.advance(i) for i in range(len(self.parts))]):
             pass
         for copy in self.done:
             copy.wait_send()
 
 
-def halving_scratch(tm_dims, region_dims, parts, rows, nodes):
-    n = len(tm_dims) + len(region_dims)
-    scratch = []
-    for _, height, _ in parts:
-        for phase in range(n):
-            scratch.append(pltpu.VMEM((2,) * (n - phase - 1) + (height, nodes), BF16))
-    copies = len(parts) * (n + len(region_dims))
+def halving_scratch(region_dims, parts, rows, nodes):
+    scratch, copies = [], 0
+    for _, height, order in parts:
+        left = sum(len(group) for group in order)
+        for group in order:
+            left -= len(group)
+            others = 2 ** len(group) - 1
+            scratch.append(pltpu.VMEM((others,) + (2,) * left + (height, nodes), BF16))
+            copies += others
+        copies += 2 ** len(region_dims) - 1
     return scratch, [
         pltpu.VMEM((2,) * len(region_dims) + (rows, nodes), BF16),
         pltpu.SemaphoreType.DMA((copies,)),
@@ -458,31 +477,25 @@
     ]
 
 
+def flat(order):
+    return [d for group in order for d in group]
+
+
 def reduce_kernel(tm_dims, region_dims, parts, *refs):
     sources, out, refs = refs[: len(parts)], refs[len(parts)], refs[len(parts) + 1 :]
     halving = Halving(sources, tm_dims, region_dims, parts, refs[:-3], *refs[-3:])
     barrier = pltpu.get_barrier_semaphore()
-    for dim in halving.dims:
-        pl.semaphore_signal(barrier, inc=1, device_id=halving.across(dim), device_id_type=MESH)
-    pl.semaphore_wait(barrier, len(halving.dims))
+    met = halving.greet(barrier)
+    pl.semaphore_wait(barrier, met)
     for i in range(len(parts)):
-        halving.begin(i)
+        halving.send_part(i)
     halving.finish()
     out[...] = halving.whole[...]
 
 
-def reduce_grads(nt, nr, grads):
-    _, width, nodes = grads.shape
-    rows = width // nr
-    tm_dims, region_dims = bit_dims(nt, nr)
-    parts = even_parts(rows, orders_of(tm_dims, region_dims))
-    grads = grads.reshape((2,) * (len(tm_dims) + len(region_dims)) + (rows, nodes))
-    dims = tm_dims + region_dims
-    sources = []
-    for start, height, order in parts:
-        moved = tuple(dims.index(d) for d in order) + (len(dims), len(dims) + 1)
-        sources.append(jnp.transpose(grads[..., start : start + height, :], moved))
-    buffers, ends = halving_scratch(tm_dims, region_dims, parts, rows, nodes)
+def reduce_grads(tm_dims, region_dims, parts, rows, sources):
+    nodes = sources[0].shape[-1]
+    buffers, ends = halving_scratch(region_dims, parts, rows, nodes)
     vmem = pl.BlockSpec(memory_space=pltpu.VMEM)
     return pl.pallas_call(
         functools.partial(reduce_kernel, tm_dims, region_dims, parts),
@@ -497,68 +510,24 @@
     )(*sources)
 
 
-def staged_parts(unit, layers, per, orders):
-    by_x, by_y, by_z = orders
-    third = per * unit // 3 // 16 * 16
-    early = per * unit - 2 * third
-    parts, stages = [], {}
-
-    def add(stage, start, height, order):
-        stages.setdefault(stage, []).append(len(parts))
-        parts.append((start, height, order))
-
-    add("output", 0, early - (early - third) // 2 // 16 * 16, by_x)
-    second = parts[0][1]
-    add("output", second, per * unit - second - third, by_y)
-    add("output", per * unit - third, third, by_z)
-    early_layers = (layers + 1) // 2
-    add(layers - early_layers, per * unit, early_layers * unit, by_z)
-    tail = (per + early_layers) * unit
-    rest = (layers + 1 - early_layers) * unit
-    cut = rest // 2 // 16 * 16
-    add("input", tail, cut, by_x)
-    add("input", tail + cut, rest - cut, by_y)
-    return parts, stages
-
-
-def step_kernel(
-    nt, tm_dims, region_dims, parts, stages,
-    cov, obs, w_input, w_filter, w_mixing, w_output, cov_grad, out,
-    scen, scored, v_input, v_filter, v_mixing, v_output, load_sem, *refs,
-):
-    edges = Edges(nt, cov, obs, *refs[:6])
-    sources, refs = refs[6 : 6 + len(parts)], refs[len(parts) :]
-    halving = Halving(sources, tm_dims, region_dims, parts, refs[6:-3], *refs[-3:])
-    barrier = pltpu.get_barrier_semaphore()
-    edges.greet(barrier)
-    for dim in region_dims:
-        pl.semaphore_signal(barrier, inc=1, device_id=halving.across(dim), device_id_type=MESH)
-    loads = {}
-    pairs = (("input", w_input, v_input), ("filter", w_filter, v_filter),
-             ("mixing", w_mixing, v_mixing), ("output", w_output, v_output))
-    for n, (name, src, dst) in enumerate(pairs):
-        loads[name] = pltpu.make_async_copy(src, dst, load_sem.at[n])
-        loads[name].start()
-    edges.own_squares()
-    pl.semaphore_wait(barrier, nt - 1 + len(region_dims))
-    edges.start()
-
+def split_parts(grads, dims, parts):
+    sources = []
+    for start, height, order in parts:
+        moved = tuple(dims.index(d) for d in flat(order)) + (len(dims), len(dims) + 1)
+        sources.append(jnp.transpose(grads[..., start : start + height, :], moved))
+    return sources
+
+
+def packed_kernel(nt, parts, cov, obs, prev_cov, next_cov, next_obs, total, *rest):
+    weights, cov_grad, sources, (scen, scored) = rest[:4], rest[4], rest[5:-2], rest[-2:]
     nodes = cov.shape[2]
-    layers, channels = w_mixing.shape[:2]
+    layers, channels = weights[2].shape[:2]
     unit = channels // nt
-    per = w_output.shape[1] // nodes // 4
+    per = weights[3].shape[1] // nodes // 4
     every = range(nt)
 
     def need(name):
-        if name == "cov":
-            edges.arrived(0, 2)
-        elif name == "obs":
-            edges.arrived(2, 3)
-        elif name == "total":
-            edges.arrived(3, None)
-            return edges.total()
-        else:
-            loads[name].wait()
+        return total[...] if name == "total" else None
 
     def put(owners, sub, at, value):
         value = value.reshape(len(owners), unit, nodes).astype(BF16)
@@ -568,7 +537,7 @@
             if low >= high:
                 continue
             for j, owner in enumerate(owners):
-                index = tuple(place[d] if d in place else owner // d[1] % 2 for d in order)
+                index = tuple(place[d] if d in place else owner // d[1] % 2 for d in flat(order))
                 index = index + (slice(low - start, high - start), slice(None))
                 source[index] = value[j, low - at * unit : high - at * unit]
 
@@ -587,63 +556,30 @@
                 for q in range(2):
                     put(owners, h * 2 + q, per + layers - 1 - l, piece[:, q])
 
-    def after(stage):
-        if stage not in ("output", layers - 1):
-            halving.round()
-        for i in stages.get(stage, []):
-            halving.begin(i)
-
     network(
-        nt, cov, obs, *edges.got, v_input, v_filter, v_mixing, v_output, cov_grad, scen, scored,
-        need, emit, after,
+        nt, cov, obs, prev_cov, next_cov, next_obs, *weights, cov_grad, scen, scored,
+        need, emit, lambda stage: None,
     )
-    halving.finish()
-    edges.sent()
-    out[...] = halving.whole[...]
-
-
-def run_step(nt, nr, cov, obs, weights):
-    seqs, rows, nodes = cov.shape
-    w_input, w_filter, w_mixing, w_output = weights
-    layers, channels = w_mixing.shape[:2]
-    unit = channels // nt
-    per = w_output.shape[1] // nodes // nr
-    tm_dims, region_dims = bit_dims(nt, nr)
-    parts, stages = staged_parts(unit, layers, per, orders_of(tm_dims, region_dims))
-    chunk = (per + layers + 1) * unit
-    buffers, ends = halving_scratch(tm_dims, region_dims, parts, chunk, nodes)
-    vmem, anywhere = pl.BlockSpec(memory_space=pltpu.VMEM), pl.BlockSpec(memory_space=pl.ANY)
-    dims = len(tm_dims) + len(region_dims)
+
+
+def run_packed(nt, dims, parts, cov, obs, edges, weights):
+    vmem = pl.BlockSpec(memory_space=pltpu.VMEM)
+    nodes = cov.shape[2]
+    sources = tuple(
+        jax.ShapeDtypeStruct((2,) * len(dims) + (height, nodes), BF16) for _, height, _ in parts
+    )
     return pl.pallas_call(
-        functools.partial(step_kernel, nt, tm_dims, region_dims, parts, stages),
-        out_shape=(
-            jax.ShapeDtypeStruct(cov.shape, BF16),
-            jax.ShapeDtypeStruct((2,) * len(region_dims) + (chunk, nodes), BF16),
-        ),
-        in_specs=[vmem] * 2 + [anywhere] * 4,
-        out_specs=(vmem, vmem),
-        scratch_shapes=network_scratch(cov, w_output)
-        + [pltpu.VMEM(w.shape, BF16) for w in weights]
-        + [
-            pltpu.SemaphoreType.DMA((4,)),
-            pltpu.VMEM((seqs, 16, nodes), BF16),
-            pltpu.VMEM((seqs, 16, nodes), BF16),
-            pltpu.VMEM((seqs, HALO, nodes), F32),
-            pltpu.VMEM((nt, seqs, 8, 128), F32),
-            pltpu.SemaphoreType.DMA((nt + 2,)),
-            pltpu.SemaphoreType.DMA((nt + 2,)),
-        ]
-        + [pltpu.VMEM((2,) * dims + (height, nodes), BF16) for _, height, _ in parts]
-        + buffers
-        + ends,
-        compiler_params=pltpu.CompilerParams(
-            collective_id=2, has_side_effects=True, vmem_limit_bytes=56 * 2**20
-        ),
-        name="step",
-    )(cov, obs, *weights)
-
-
-def unpack_kernel(cov_grad, whole, o_cov, o_input, o_filter, o_mixing, o_output):
+        functools.partial(packed_kernel, nt, parts),
+        out_shape=(jax.ShapeDtypeStruct(cov.shape, BF16),) + sources,
+        in_specs=[vmem] * 10,
+        out_specs=(vmem,) * (1 + len(sources)),
+        scratch_shapes=network_scratch(cov, weights[3]),
+        compiler_params=pltpu.CompilerParams(vmem_limit_bytes=56 * 2**20),
+        name="network",
+    )(cov, obs, *edges, *weights)
+
+
+def unpack_kernel(whole, o_input, o_filter, o_mixing, o_output):
     unit, nodes = o_input.shape
     layers = o_filter.shape[0]
     scenarios = o_output.shape[1] // nodes
@@ -652,7 +588,6 @@
     def piece(sub, at):
         return whole[sub // 2, sub % 2, at * unit : (at + 1) * unit, :]
 
-    o_cov[...] = cov_grad[...]
     for s in range(scenarios):
         o_output[:, s * nodes : (s + 1) * nodes] = piece(s // per, s % per)
     for l in range(layers):
@@ -665,16 +600,15 @@
     o_input[...] = piece(layers, per + layers)
 
 
-def unpack(cov_grad, summed, shapes):
+def unpack(summed, shapes):
     vmem = pl.BlockSpec(memory_space=pltpu.VMEM)
-    shapes = (cov_grad.shape,) + shapes
     return pl.pallas_call(
         unpack_kernel,
         out_shape=tuple(jax.ShapeDtypeStruct(s, BF16) for s in shapes),
-        in_specs=[vmem] * 2,
+        in_specs=[vmem],
         out_specs=(vmem,) * len(shapes),
         name="unpack",
-    )(cov_grad, summed)
+    )(summed)
 
 
 def per_device(nt, nr, cov, obs, w_input, w_filter, w_mixing, w_output):
@@ -686,15 +620,23 @@
     shapes = (
         (unit, nodes), (layers, 2 * unit, 2 * channels), (layers, unit, channels), (unit, scenarios * nodes)
     )
+    tm_dims, region_dims = bit_dims(nt, nr)
+    dims = tm_dims + region_dims
+    rows = sum(w.size for w in weights) // nt // nodes // nr
+    parts = even_parts(rows, orders_of(tm_dims, region_dims))
+    edges = exchange_edges(nt, cov, obs)
     if unit % 16 == 0 and nr == 4 and layers == 3 and scenarios == 16 and channels == nodes:
-        return tuple(unpack(*run_step(nt, nr, cov, obs, weights), shapes))
-    edges = exchange_edges(nt, cov, obs)
+        cov_grad, *sources = run_packed(nt, dims, parts, cov, obs, edges, weights)
+        summed = reduce_grads(tm_dims, region_dims, parts, rows, sources)
+        return (cov_grad, *unpack(summed, shapes))
     cov_grad, *grads = run_network(nt, cov, obs, edges, weights)
     sources = tuple(
         jnp.moveaxis(g.reshape(g.shape[:-2] + (nt, -1) + g.shape[-1:]), -3, 0) for g in grads
     )
-    flat = jnp.concatenate([s.reshape(nt, -1) for s in sources], axis=1).reshape(nt, -1, nodes)
-    summed = reduce_grads(nt, nr, flat).reshape(-1)
+    together = jnp.concatenate([s.reshape(nt, -1) for s in sources], axis=1)
+    together = together.reshape((2,) * len(dims) + (rows, nodes))
+    summed = reduce_grads(tm_dims, region_dims, parts, rows, split_parts(together, dims, parts))
+    summed = summed.reshape(-1)
     outs, first = [], 0
     for source, shape in zip(sources, shapes):
         size = source.size // nt

time: 72 us -> 72.4 us (level)
    pallas_call x1 -> x3, Pallas kernels: 69.3 us -> 69.7 us  [the longest x1 37.5 us: reduce_grads(): pl.pallas_call(functools.partial(reduce_kernel, tm_dims, region_dims, par...]
where the time goes in v5:
time: 72.4 us; the launch traced here: 72.2 us
  Pallas kernels  71.6 us (99%)
    pallas_call x1, Pallas kernels, reduce_grads(): pl.pallas_call(functools.partial(reduce_kernel, tm_dims, region_dims, par...  37.5 us
    pallas_call x1, Pallas kernels, run_packed(): pl.pallas_call(functools.partial(packed_kernel, nt, parts), out_shape=(ja...  21.4 us
    pallas_call x1, Pallas kernels, exchange_edges(): pl.pallas_call(functools.partial(edges_kernel, nt), out_shape=(edge, edge...  10.8 us
    pallas_call x1, Pallas kernels, unpack(): pl.pallas_call(unpack_kernel, out_shape=tuple((jax.ShapeDtypeStruct(s, BF...  1.83 us

profile of v5, /device:TPU:0, one launch (start us, length us, event | category | flops | bytes accessed | tf_op | source)
XLA Modules:
  0.0 72.2 jit_solution(4322592847115105506)
XLA Ops:
  0.6 10.8 %edges.1 = (bf16[2,16,256]{2,1,0:T(8,128)(2,1)}, bf16[2,16,256]{2,1,0:T(8,128)(2,1)}, f32[2,8,256]{2,1,0:T(8,128)}, f32[2,8,128]{2,1,0:T(8,128)}) custom-call(bf16[2,128,256]{2,1,0:T(8,128)(2,1)} %cov.3, f32[2,128,256]{2,1,0:T(8,128)} %obs.3), custom_call_target="tpu_custom_call" | custom-call | tf_op jit(solution)/shard_map/edges/pallas_call | solution.py:95
  11.4 21.4 %network.1 = (bf16[2,128,256]{2,1,0:T(8,128)(2,1)}, bf16[2,2,2,2,2,32,256]{6,5,4,3,2,1,0:T(8,128)(2,1)}, bf16[2,2,2,2,2,48,256]{6,5,4,3,2,1,0:T(8,128)(2,1)}, bf...) custom-call(bf16[2,128,256]{2,1,0:T(8,128)(2,1)} %cov.3, ...), custom_call_target="tpu_custom_call" | custom-call | tf_op jit(solution)/shard_map/network/pallas_call | solution.py:571
  32.8 37.5 %reduce.1.whole = bf16[2,2,256,256]{3,2,1,0:T(8,128)(2,1)} custom-call(bf16[2,2,2,2,2,32,256]{6,5,4,3,2,1,0:T(8,128)(2,1)} %get-tuple-element.25.refs_0_, bf16[2,2,2,2,2,48,256]{6,5,4,3,2,1,0:T(8,128)(2,1)} %get-tuple-element.26.refs_1_, bf16[2,2,2,2,2,48,256]{6,5,4,3,2,1,0:T(8,128)(2,1)} %get-tuple-element.27.refs_2_, ...), custom_call_target="tpu_custom_call" | custom-call | tf_op jit(solution)/shard_map/reduce/pallas_call | solution.py:500
  70.4 1.8 %unpack.1 = (bf16[32,256]{1,0:T(8,128)(2,1)}, bf16[3,64,512]{2,1,0:T(8,128)(2,1)}, bf16[3,32,256]{2,1,0:T(8,128)(2,1)}, bf16[32,4096]{1,0:T(8,128)(2,1)}) custom-call(bf16[2,2,256,256]{3,2,1,0:T(8,128)(2,1)} %reduce.1.whole), custom_call_target="tpu_custom_call" | custom-call | tf_op jit(solution)/shard_map/unpack/pallas_call | solution.py:605

commit v6 on v4

--- a/solution.py
+++ b/solution.py
@@ -588,8 +588,6 @@
                     put(owners, h * 2 + q, per + layers - 1 - l, piece[:, q])
 
     def after(stage):
-        if stage not in ("output", layers - 1):
-            halving.round()
         for i in stages.get(stage, []):
             halving.begin(i)
 

time: 72 us -> 61.2 us (0.85)
  Pallas kernels: 71.2 us -> 60.4 us
    pallas_call x1, Pallas kernels: 69.3 us -> 58.5 us  [run_step(): pl.pallas_call(functools.partial(step_kernel, nt, tm_dims, region_dims, p...]
where the time goes in v6:
time: 61.2 us; the launch traced here: 61.1 us
  Pallas kernels  60.4 us (99%)
  between operations  0.64 us (1%)
    pallas_call x1, Pallas kernels, run_step(): pl.pallas_call(functools.partial(step_kernel, nt, tm_dims, region_dims, p...  58.5 us
    pallas_call x1, Pallas kernels, unpack(): pl.pallas_call(unpack_kernel, out_shape=tuple((jax.ShapeDtypeStruct(s, BF...  1.95 us

profile of v6, /device:TPU:0, one launch (start us, length us, event | category | flops | bytes accessed | tf_op | source)
XLA Modules:
  0.0 61.1 jit_solution(17376286662469519434)
XLA Ops:
  0.6 58.5 %step.1 = (bf16[2,128,256]{2,1,0:T(8,128)(2,1)}, bf16[2,2,256,256]{3,2,1,0:T(8,128)(2,1)}) custom-call(bf16[2,128,256]{2,1,0:T(8,128)(2,1)} %cov.1, f32[2,128,256]{2,1,0:T(8,128)} %obs.1, bf16[256,256]{1,0:T(8,128)(2,1)} %w_input.1, bf16[3,512,512]{2,1,0:T(8,128)(2,1)} %w_filter.1, bf16[3,256,256]{2,1,0:T(8,128)(2,1)} %w_mixing.1, bf16[256,4096]{1,0:T(8,128)(2,1)} %w_output.1), custom_call_target="tpu_custom_call" | custom-call | tf_op jit(solution)/shard_map/step/pallas_call | solution.py:615
  59.1 2.0 %unpack.1 = (bf16[2,128,256]{2,1,0:T(8,128)(2,1)}, bf16[32,256]{1,0:T(8,128)(2,1)}, bf16[3,64,512]{2,1,0:T(8,128)(2,1)}, bf16[3,32,256]{2,1,0:T(8,128)(2,1)}, bf16[32,4096]{1,0:T(8,128)(2,1)}) custom-call(bf16[2,128,256]{2,1,0:T(8,128)(2,1)} %get-tuple-element.7.cov_grad, bf16[2,2,256,256]{3,2,1,0:T(8,128)(2,1)} %get-tuple-element.8.whole), custom_call_target="tpu_custom_call" | custom-call | tf_op jit(solution)/shard_map/unpack/pallas_call | solution.py:669

commit v7 on v6

--- a/solution.py
+++ b/solution.py
@@ -588,6 +588,9 @@
                     put(owners, h * 2 + q, per + layers - 1 - l, piece[:, q])
 
     def after(stage):
+        if stage == 0:
+            for i in stages["output"]:
+                halving.advance(i)
         for i in stages.get(stage, []):
             halving.begin(i)
 

time: 61.2 us -> 66 us (1.078)
  Pallas kernels: 60.4 us -> 65.2 us
    pallas_call x1, Pallas kernels: 58.5 us -> 63.3 us  [run_step(): pl.pallas_call(functools.partial(step_kernel, nt, tm_dims, region_dims, p...]
where the time goes in v7:
time: 66 us; the launch traced here: 65.9 us
  Pallas kernels  65.2 us (99%)
    pallas_call x1, Pallas kernels, run_step(): pl.pallas_call(functools.partial(step_kernel, nt, tm_dims, region_dims, p...  63.3 us
    pallas_call x1, Pallas kernels, unpack(): pl.pallas_call(unpack_kernel, out_shape=tuple((jax.ShapeDtypeStruct(s, BF...  1.95 us

profile of v7, /device:TPU:0, one launch (start us, length us, event | category | flops | bytes accessed | tf_op | source)
XLA Modules:
  0.0 65.9 jit_solution(18138382646654465962)
XLA Ops:
  0.6 63.3 %step.1 = (bf16[2,128,256]{2,1,0:T(8,128)(2,1)}, bf16[2,2,256,256]{3,2,1,0:T(8,128)(2,1)}) custom-call(bf16[2,128,256]{2,1,0:T(8,128)(2,1)} %cov.1, f32[2,128,256]{2,1,0:T(8,128)} %obs.1, bf16[256,256]{1,0:T(8,128)(2,1)} %w_input.1, bf16[3,512,512]{2,1,0:T(8,128)(2,1)} %w_filter.1, bf16[3,256,256]{2,1,0:T(8,128)(2,1)} %w_mixing.1, bf16[256,4096]{1,0:T(8,128)(2,1)} %w_output.1), custom_call_target="tpu_custom_call" | custom-call | tf_op jit(solution)/shard_map/step/pallas_call | solution.py:618
  63.9 2.0 %unpack.1 = (bf16[2,128,256]{2,1,0:T(8,128)(2,1)}, bf16[32,256]{1,0:T(8,128)(2,1)}, bf16[3,64,512]{2,1,0:T(8,128)(2,1)}, bf16[3,32,256]{2,1,0:T(8,128)(2,1)}, bf16[32,4096]{1,0:T(8,128)(2,1)}) custom-call(bf16[2,128,256]{2,1,0:T(8,128)(2,1)} %get-tuple-element.7.cov_grad, bf16[2,2,256,256]{3,2,1,0:T(8,128)(2,1)} %get-tuple-element.8.whole), custom_call_target="tpu_custom_call" | custom-call | tf_op jit(solution)/shard_map/unpack/pallas_call | solution.py:672
